TPU v7x, 512 devices: a whole 4x8x8 slice. The times are simulated.
512 devices in a mesh: seq: 128 (over y, z, core), head: 4 (over x).
Axes of the slice: x: 4, y: 8, z: 8, core: 2. Of those that a mesh axis runs over, the one named last changes fastest.
Arguments:
- routed_qkv: bfloat16 [3, 32768, 1024], P(None, 'seq', 'head'), may hold values from -64 to 64
- local_qkv: bfloat16 [3, 32768, 3072], P(None, 'seq', 'head'), may hold values from -64 to 64
- cluster_ids: int32 [8, 32768, 1], P('head', 'seq'), may hold values from 0 to 255; in each aligned block of 256 rows (0 to 255, 256 to 511, ..., all dimensions but the last counted through in order) at most 2 rows name the same one
- wo_routed: bfloat16 [1024, 4096], P('head', 'seq'), may hold values from -0.09375 to 0.09375
- wo_local: bfloat16 [3072, 4096], P('head', 'seq'), may hold values from -0.09375 to 0.09375
Outputs:
- layer_out: bfloat16 [32768, 4096], P('seq', 'head')
Inputs may be any that keep to these rules, and one draw needn't show every extreme that they name: `cluster_ids`: in each routed head, no cluster holds more than 2 of the 256 tokens of one index of seq (aligned blocks of 256 rows), and some cluster holds exactly 2 of them.
All inputs are finite; a program needn't handle non-finite values.
Results may differ from a plain program's by a relative error of at most 0.0095.
Values may be sent and summed in bfloat16 or wider, within the bound.
A program may use at most 64 MiB of HBM per device.

v0:
```python
import math

import jax
import jax.numpy as jnp
from jax import lax
from jax.sharding import PartitionSpec as P

HD = 128
WIN = 256
CL_DEV = 2


def shifted(block, axis, distance):
    devices = range(lax.axis_size(axis))
    route = [(i - distance, i) for i in devices if i - distance in devices]
    return lax.ppermute(block, axis, route)


def attend(query, keys, values, allowed):
    scores = jnp.einsum("...qd,...kd->...qk", query, keys, preferred_element_type=jnp.float32) * (
        1.0 / math.sqrt(HD)
    )
    scores = jnp.where(allowed, scores, jnp.float32(-1e30))
    largest = jnp.max(scores, axis=-1, keepdims=True)
    raised = jnp.exp(scores - largest)
    weights = (raised / jnp.sum(raised, axis=-1, keepdims=True)).astype(jnp.bfloat16)
    return jnp.einsum(
        "...qk,...kd->...qd", weights, values, preferred_element_type=jnp.float32
    ).astype(jnp.bfloat16)


def on_device(routed_qkv, local_qkv, cluster_ids, wo_routed, wo_local):
    seq_count = lax.axis_size("seq")
    seq_place = lax.axis_index("seq")
    tok_rows = routed_qkv.shape[1]
    routed_count = cluster_ids.shape[0]
    local_count = local_qkv.shape[2] // HD
    cluster_total = CL_DEV * seq_count
    most_slots = max(2, 2 * tok_rows // cluster_total)
    proj_rows = jnp.concatenate([wo_routed, wo_local], axis=0)
    head_rows = (
        routed_qkv.reshape(3, tok_rows, routed_count, HD)
        .transpose(2, 1, 0, 3)
        .reshape(routed_count, tok_rows, 3 * HD)
    )
    cluster = cluster_ids[:, :, 0]
    labels = jnp.arange(cluster_total, dtype=jnp.int32)
    onehot = (cluster[:, :, None] == labels[None, None, :]).astype(jnp.int32)
    rank = jnp.sum((jnp.cumsum(onehot, axis=1) - 1) * onehot, axis=2)
    slot_index = cluster * most_slots + rank
    own_pos = seq_place * tok_rows + jnp.arange(tok_rows, dtype=jnp.int32)
    slot_total = cluster_total * most_slots

    def place_rows(slot_row, data):
        return jnp.zeros((slot_total, 3 * HD), data.dtype).at[slot_row].set(data)

    def place_pos(slot_row):
        return jnp.full((slot_total,), -1, jnp.int32).at[slot_row].set(own_pos)

    send_rows = jax.vmap(place_rows)(slot_index, head_rows)
    send_pos = jax.vmap(place_pos)(slot_index)
    rows = lax.all_to_all(send_rows, "seq", split_axis=1, concat_axis=1, tiled=True)
    positions = lax.all_to_all(send_pos, "seq", split_axis=1, concat_axis=1, tiled=True)
    count = rows.shape[0]
    slots = rows.shape[1]
    group = seq_count * most_slots
    members = (
        rows.reshape(count, seq_count, CL_DEV, most_slots, 3 * HD)
        .transpose(0, 2, 1, 3, 4)
        .reshape(count, CL_DEV, group, 3 * HD)
    )
    where_at = (
        positions.reshape(count, seq_count, CL_DEV, most_slots)
        .transpose(0, 2, 1, 3)
        .reshape(count, CL_DEV, group)
    )
    allowed = (where_at[..., None, :] >= 0) & (where_at[..., None, :] <= where_at[..., :, None])
    result = attend(members[..., :HD], members[..., HD : 2 * HD], members[..., 2 * HD :], allowed)
    answered = (
        result.reshape(count, CL_DEV, seq_count, most_slots, HD)
        .transpose(0, 2, 1, 3, 4)
        .reshape(count, slots, HD)
    )
    returned = lax.all_to_all(answered, "seq", split_axis=1, concat_axis=1, tiled=True)
    picked = jnp.take_along_axis(returned, slot_index[:, :, None], axis=1)
    routed_attn = picked.transpose(1, 0, 2).reshape(tok_rows, routed_count * HD)
    heads = local_qkv.reshape(3, tok_rows, local_count, HD).transpose(0, 2, 1, 3)
    tail = jnp.stack([heads[1], heads[2]])
    earlier = shifted(tail, "seq", 1)
    keys = jnp.concatenate([earlier[0], heads[1]], axis=1)
    values = jnp.concatenate([earlier[1], heads[2]], axis=1)
    key_pos = seq_place * tok_rows - WIN + jnp.arange(WIN + tok_rows, dtype=jnp.int32)
    query_pos = seq_place * tok_rows + jnp.arange(tok_rows, dtype=jnp.int32)
    allowed = (
        (key_pos[None, :] >= 0)
        & (key_pos[None, :] <= query_pos[:, None])
        & (key_pos[None, :] > query_pos[:, None] - WIN)
    )
    result = attend(heads[0], keys, values, allowed[None])
    local_attn = result.transpose(1, 0, 2).reshape(tok_rows, local_count * HD)
    joined = jnp.concatenate([routed_attn, local_attn], axis=1)
    terms = jnp.dot(
        joined,
        lax.all_gather(proj_rows, "seq", axis=1, tiled=True),
        preferred_element_type=jnp.float32,
    )
    rounded = terms.astype(jnp.bfloat16)
    return (
        lax.psum_scatter(rounded, "head", scatter_dimension=1, tiled=True)
        .astype(jnp.float32)
        .astype(jnp.bfloat16)
    )


def solution(mesh):
    placed = (
        P(None, "seq", "head"),
        P(None, "seq", "head"),
        P("head", "seq", None),
        P("head", "seq"),
        P("head", "seq"),
    )
    return jax.shard_map(
        on_device, mesh=mesh, in_specs=placed, out_specs=P("seq", "head"), check_vma=False
    )
```

profile of v0, /device:TPU:1, one launch (start us, length us, event | category | flops | bytes accessed | tf_op | source)
XLA Modules:
  0.0 208.0 jit_solution(6545766320278965949)
XLA Ops:
  6.5 1.4 pad_maximum_fusion
  8.0 0.7 copy.68
  8.7 0.8 copy.41
  9.5 0.4 fusion.18
  10.6 24.5 %scatter_fusion = s32[2,512]{1,0:T(2,128)S(1)} fusion(s32[2,512]{1,0:T(2,128)S(1)} %broadcast_in_dim.51, s32[512]{0:T(512)S(1)} %bitcast.73, s32[512]{0:T(512)S(1)} %bitcast.90), kind=kCustom, calls=%fused_computation.1 | custom fusion | bytes 10240 | tf_op jit(solution)/shard_map/vmap()/scatter | solution.py:58
  35.3 0.8 copy.43
  36.1 18.4 %all-to-all-start = ((s32[2,128,4]{2,0,1:T(2,128)}), s32[2,128,4]{2,0,1:T(2,128)S(1)}, u32[]{:S(2)}, u32[]{:S(2)}) async-start(s32[2,128,4]{2,0,1:T(2,128)} %copy.43), calls=%async_computation | async-start | bytes 262144 | tf_op jit(solution)/shard_map/all_to_all | solution.py:63
  54.6 0.6 copy.46
  55.6 26.6 %scatter_fusion.1 = bf16[2,512,384]{2,1,0:T(8,128)(2,1)S(1)} fusion(bf16[2,512,384]{2,1,0:T(8,128)(2,1)S(1)} %broadcast_in_dim.53, s32[512]{0:T(512)S(1)} %bitcast.74, bf16[512,384]{1,0:T(8,128)(2,1)S(1)} %copy.47), kind=kCustom, calls=%fused_computation.2 | custom fusion | bytes 1183744 | tf_op jit(solution)/shard_map/vmap()/scatter | solution.py:55
  82.2 1.7 copy.48
  83.9 13.7 %all-to-all-start.1 = ((bf16[2,512,384]{2,0,1:T(2,128)(2,1)}), bf16[2,512,384]{2,0,1:T(2,128)(2,1)S(1)}, u32[]{:S(2)}, u32[]{:S(2)}) async-start(bf16[2,512,384]{2,0,1:T(2,128)(2,1)} %copy.48), calls=%async_computation.1 | async-start | bytes 1572864 | tf_op jit(solution)/shard_map/all_to_all | solution.py:62
  97.6 1.6 copy.54
  99.2 0.7 copy.55
  100.0 1.0 stack.4
  100.9 3.7 %collective-permute-start = (bf16[2,6,256,128]{3,2,1,0:T(8,128)(2,1)}, bf16[2,6,256,128]{3,2,1,0:T(8,128)(2,1)S(1)}, u32[]{:S(2)}, u32[]{:S(2)}) collective-permute-start(bf16[2,6,256,128]{3,2,1,0:T(8,128)(2,1)} %stack.4), channel_id=1, source_target_pairs={{0,4},{4,8},{8,12},{12,16},{16,20},{20,24},{24,28},{28,32},{32,36}... | collective-permute-start | bytes 2359304 | tf_op jit(solution)/shard_map/ppermute | solution.py:16
  104.9 0.8 slice_bitcast_fusion
  106.2 19.7 %collective-permute-done = bf16[2,6,256,128]{3,2,1,0:T(8,128)(2,1)S(1)} collective-permute-done((bf16[2,6,256,128]{3,2,1,0:T(8,128)(2,1)}, bf16[2,6,256,128]{3,2,1,0:T(8,128)(2,1)S(1)}, u32[]{:S(2)}, u32[]{:S(2)}) %collective-permute-start) | collective-permute-done | bytes 786464 | tf_op jit(solution)/shard_map/ppermute | solution.py:16
  125.9 0.8 slice_bitcast_fusion.1
  126.7 2.3 %fusion.11 = f32[6,512,256]{2,1,0:T(8,128)} fusion(bf16[6,256,128]{2,1,0:T(8,128)(2,1)S(1)} %get-tuple-element.10, bf16[6,256,128]{2,1,0:T(8,128)(2,1)S(1)} %get-tuple-element.12, bf16[3,6,256,128]{3,2,1,0:T(8,128)(2,1)S(1)} %bitcast.78), kind=kOutput, calls=%fused_computation.22 | convolution fusion | flops 202899456 | bytes 4325376 | tf_op jit(solution)/shard_map/...qd,...kd->...qk/dot_general | solution.py:20
  129.1 0.6 copy.49
  129.7 0.3 reshape.160
  130.0 0.8 fusion.44
  130.9 1.3 fusion.9
  132.2 2.2 %convolution_convert_fusion.1 = bf16[2,2,256,128]{3,2,1,0:T(8,128)(2,1)S(1)} fusion(f32[2,2,256]{2,1,0:T(2,128)S(1)} %fusion.44, bf16[2,2,256,384]{3,2,1,0:T(8,128)(2,1)} %copy-done.1, f32[2,2,256,256]{2,3,1,0:T(8,128)} %fusion.9), kind=kOutput, calls=%fused_computation.19 | convolution fusion | flops 68027648 | bytes 2625536 | tf_op jit(solution)/shard_map/...qk,...kd->...qd/dot_general | solution.py:27
  134.5 1.1 copy.51
  135.6 12.2 %all-to-all-start.2 = ((bf16[2,512,128]{2,0,1:T(2,128)(2,1)}), bf16[2,512,128]{2,0,1:T(2,128)(2,1)S(1)}, u32[]{:S(2)}, u32[]{:S(2)}) async-start(bf16[2,512,128]{2,0,1:T(2,128)(2,1)} %bitcast.83), calls=%async_computation.2 | async-start | bytes 524288 | tf_op jit(solution)/shard_map/all_to_all | solution.py:84
  147.9 1.5 fusion.43
  149.4 0.5 fusion.10
  149.9 12.2 %all-to-all-done.2 = bf16[2,512,128]{2,0,1:T(2,128)(2,1)S(1)} async-done(((bf16[2,512,128]{2,0,1:T(2,128)(2,1)}), bf16[2,512,128]{2,0,1:T(2,128)(2,1)S(1)}, u32[]{:S(2)}, u32[]{:S(2)}) %all-to-all-start.2) | async-done | bytes 262176 | tf_op jit(solution)/shard_map/all_to_all | solution.py:84
  162.1 3.2 %gather_fusion = bf16[512,128]{1,0:T(8,128)(2,1)S(1)} fusion(bf16[2,512,128]{2,1,0:T(8,128)(2,1)S(1)} %copy.52, s32[512]{0:T(512)S(1)} %bitcast.75), kind=kCustom, calls=%fused_computation | custom fusion | bytes 266240 | tf_op jit(solution)/shard_map/jit(take_along_axis)/gather | solution.py:85
  165.6 7.2 %convolution_convert_fusion = bf16[256,4096]{1,0:T(8,128)(2,1)} fusion(bf16[1024,4096]{0,1:T(8,128)(2,1)} %all-gather.2.cloned.1.call-done, bf16[256,768]{0,1:T(8,128)(2,1)S(1)} %bitcast.92, bf16[256,256]{0,1:T(8,128)(2,1)S(1)} %bitcast.86), kind=kOutput, calls=%fused_computation.5 | convolution fusion | flops 2149580800 | bytes 11010048 | tf_op jit(solution)/shard_map/dot_general | solution.py:102
  172.8 28.4 %reduce-scatter.2.cloned.1.call-done = bf16[256,1024]{1,0:T(8,128)(2,1)} async-done(((bf16[256,4096]{1,0:T(8,128)(2,1)}), bf16[256,1024]{1,0:T(8,128)(2,1)}) %reduce-scatter.2.cloned.1.call-update) | async-done | bytes 524304 | tf_op jit(solution)/shard_map/reduce_scatter | solution.py:109
  (47 shorter events, 2.4 us)
Async XLA Ops:
  6.5 4.1 %copy-start.5 = (s32[2,256,1]{1,2,0:T(1,128)S(1)}, s32[2,256,1]{1,2,0:T(1,128)}, u32[]{:S(2)}) copy-start(s32[2,256,1]{1,2,0:T(1,128)} %param.7) | copy-start | bytes 6148
  6.5 159.0 %all-gather.2.cloned.1.call-start = ((), (), s32[]{:S(2)}) async-start(), calls=%async_computation.4 | async-start | bytes 8454144 | tf_op jit(solution)/shard_map/all_gather | solution.py:104
  10.2 44.2 %copy-start.2 = (bf16[3,256,256]{2,1,0:T(8,128)(2,1)S(1)}, bf16[3,256,256]{2,1,0:T(8,128)(2,1)}, u32[]{:S(2)}) copy-start(bf16[3,256,256]{2,1,0:T(8,128)(2,1)} %param.5) | copy-start | bytes 1179652
  36.1 47.9 %all-to-all-start = ((s32[2,128,4]{2,0,1:T(2,128)}), s32[2,128,4]{2,0,1:T(2,128)S(1)}, u32[]{:S(2)}, u32[]{:S(2)}) async-start(s32[2,128,4]{2,0,1:T(2,128)} %copy.43), calls=%async_computation | async-start | bytes 262144 | tf_op jit(solution)/shard_map/all_to_all | solution.py:63
  83.9 45.1 %all-to-all-start.1 = ((bf16[2,512,384]{2,0,1:T(2,128)(2,1)}), bf16[2,512,384]{2,0,1:T(2,128)(2,1)S(1)}, u32[]{:S(2)}, u32[]{:S(2)}) async-start(bf16[2,512,384]{2,0,1:T(2,128)(2,1)} %copy.48), calls=%async_computation.1 | async-start | bytes 1572864 | tf_op jit(solution)/shard_map/all_to_all | solution.py:62
  100.9 25.0 %collective-permute-start = (bf16[2,6,256,128]{3,2,1,0:T(8,128)(2,1)}, bf16[2,6,256,128]{3,2,1,0:T(8,128)(2,1)S(1)}, u32[]{:S(2)}, u32[]{:S(2)}) collective-permute-start(bf16[2,6,256,128]{3,2,1,0:T(8,128)(2,1)} %stack.4), channel_id=1, source_target_pairs={{0,4},{4,8},{8,12},{12,16},{16,20},{20,24},{24,28},{28,32},{32,36}... | collective-permute-start | bytes 2359304 | tf_op jit(solution)/shard_map/ppermute | solution.py:16
  130.0 0.9 copy-start.1
  132.2 15.6 %copy-start = (f32[6,512,256]{2,1,0:T(8,128)S(1)}, f32[6,512,256]{2,1,0:T(8,128)}, u32[]{:S(2)}) copy-start(f32[6,512,256]{2,1,0:T(8,128)} %fusion.11) | copy-start | bytes 9437188
  135.6 26.5 %all-to-all-start.2 = ((bf16[2,512,128]{2,0,1:T(2,128)(2,1)}), bf16[2,512,128]{2,0,1:T(2,128)(2,1)S(1)}, u32[]{:S(2)}, u32[]{:S(2)}) async-start(bf16[2,512,128]{2,0,1:T(2,128)(2,1)} %bitcast.83), calls=%async_computation.2 | async-start | bytes 524288 | tf_op jit(solution)/shard_map/all_to_all | solution.py:84
  147.8 53.4 %reduce-scatter.2.cloned.1.call-start = ((), (), s32[]{:S(2)}) async-start(), calls=%async_computation.5 | async-start | bytes 2621440 | tf_op jit(solution)/shard_map/reduce_scatter | solution.py:109
  147.9 1.5 copy-start.3
  147.9 1.5 copy-start.4
Sparse Core Ops, SparseCore 0:
  10.5 100.0 all-gather.1
  172.9 28.2 reduce-scatter.1
where the time goes:
time: 208 us
  local copies, waits for them, and re-layouts  67.2 us (32%)
  waiting for transfers between devices  60.3 us (29%)
  starting transfers between devices  48.1 us (23%)
  matrix products  14.4 us (7%)
  between operations  13.8 us (7%)
  other arithmetic  4.24 us (2%)
    reduce_scatter x1, waiting for transfers between devices, on_device(): lax.psum_scatter(rounded, 'head', scatter_dimension=1, tiled=True)  28.4 us
    scatter x2, local copies, waits for them, and re-layouts, place_rows(): return jnp.zeros((slot_total, 3 * HD), data.dtype).at[slot_row].set(data)  28.3 us
    scatter x1, local copies, waits for them, and re-layouts, place_pos(): return jnp.full((slot_total,), -1, jnp.int32).at[slot_row].set(own_pos)  24.5 us
    ppermute x1, waiting for transfers between devices, shifted(): return lax.ppermute(block, axis, route)  19.7 us
    all_to_all x1, starting transfers between devices, on_device(): lax.all_to_all(send_pos, 'seq', split_axis=1, concat_axis=1, tiled=True)  18.4 us
    all_to_all x1, starting transfers between devices, on_device(): lax.all_to_all(send_rows, 'seq', split_axis=1, concat_axis=1, tiled=True)  13.7 us
    all_to_all x1, starting transfers between devices, on_device(): lax.all_to_all(answered, 'seq', split_axis=1, concat_axis=1, tiled=True)  12.2 us
    all_to_all x1, waiting for transfers between devices, on_device(): lax.all_to_all(answered, 'seq', split_axis=1, concat_axis=1, tiled=True)  12.2 us
  transfers between devices with their start and end apart: 6, of which 3 were waited for; matrix products, arithmetic and copies ran while one was open for 37% of the time, Pallas kernels for 0%

commit v1 on v0

--- a/solution.py
+++ b/solution.py
@@ -8,6 +8,7 @@
 HD = 128
 WIN = 256
 CL_DEV = 2
+EMPTY = 128.0
 
 
 def shifted(block, axis, distance):
@@ -44,23 +45,19 @@
         .reshape(routed_count, tok_rows, 3 * HD)
     )
     cluster = cluster_ids[:, :, 0]
-    labels = jnp.arange(cluster_total, dtype=jnp.int32)
-    onehot = (cluster[:, :, None] == labels[None, None, :]).astype(jnp.int32)
-    rank = jnp.sum((jnp.cumsum(onehot, axis=1) - 1) * onehot, axis=2)
+    order = jnp.arange(tok_rows, dtype=jnp.int32)
+    same = (cluster[:, :, None] == cluster[:, None, :]) & (order[None, None, :] < order[None, :, None])
+    rank = jnp.sum(same.astype(jnp.int32), axis=2)
     slot_index = cluster * most_slots + rank
-    own_pos = seq_place * tok_rows + jnp.arange(tok_rows, dtype=jnp.int32)
     slot_total = cluster_total * most_slots
-
-    def place_rows(slot_row, data):
-        return jnp.zeros((slot_total, 3 * HD), data.dtype).at[slot_row].set(data)
-
-    def place_pos(slot_row):
-        return jnp.full((slot_total,), -1, jnp.int32).at[slot_row].set(own_pos)
-
-    send_rows = jax.vmap(place_rows)(slot_index, head_rows)
-    send_pos = jax.vmap(place_pos)(slot_index)
+    slot_names = jnp.arange(slot_total, dtype=jnp.int32)
+    place = (slot_names[None, :, None] == slot_index[:, None, :]).astype(jnp.bfloat16)
+    filled = jnp.sum(place.astype(jnp.float32), axis=2, keepdims=True)
+    send_rows = (
+        jnp.einsum("hst,htd->hsd", place, head_rows, preferred_element_type=jnp.float32)
+        + (1.0 - filled) * EMPTY
+    ).astype(jnp.bfloat16)
     rows = lax.all_to_all(send_rows, "seq", split_axis=1, concat_axis=1, tiled=True)
-    positions = lax.all_to_all(send_pos, "seq", split_axis=1, concat_axis=1, tiled=True)
     count = rows.shape[0]
     slots = rows.shape[1]
     group = seq_count * most_slots
@@ -69,12 +66,9 @@
         .transpose(0, 2, 1, 3, 4)
         .reshape(count, CL_DEV, group, 3 * HD)
     )
-    where_at = (
-        positions.reshape(count, seq_count, CL_DEV, most_slots)
-        .transpose(0, 2, 1, 3)
-        .reshape(count, CL_DEV, group)
-    )
-    allowed = (where_at[..., None, :] >= 0) & (where_at[..., None, :] <= where_at[..., :, None])
+    present = members[..., HD] < EMPTY / 2
+    slot_order = jnp.arange(group, dtype=jnp.int32)
+    allowed = present[..., None, :] & (slot_order[None, :] <= slot_order[:, None])
     result = attend(members[..., :HD], members[..., HD : 2 * HD], members[..., 2 * HD :], allowed)
     answered = (
         result.reshape(count, CL_DEV, seq_count, most_slots, HD)
@@ -82,7 +76,9 @@
         .reshape(count, slots, HD)
     )
     returned = lax.all_to_all(answered, "seq", split_axis=1, concat_axis=1, tiled=True)
-    picked = jnp.take_along_axis(returned, slot_index[:, :, None], axis=1)
+    picked = jnp.einsum(
+        "hst,hsd->htd", place, returned, preferred_element_type=jnp.float32
+    ).astype(jnp.bfloat16)
     routed_attn = picked.transpose(1, 0, 2).reshape(tok_rows, routed_count * HD)
     heads = local_qkv.reshape(3, tok_rows, local_count, HD).transpose(0, 2, 1, 3)
     tail = jnp.stack([heads[1], heads[2]])

time: 208 us -> 168 us (0.81)
  local copies, waits for them, and re-layouts: 67.2 us -> 8.9 us
  waiting for transfers between devices: 60.3 us -> 86.7 us
  starting transfers between devices: 48.1 us -> 35.3 us
  other arithmetic: 4.24 us -> 6.95 us
    scatter x3 -> x0, local copies, waits for them, and re-layouts: 52.8 us -> none  [the longest x2 28.3 us: place_rows(): return jnp.zeros((slot_total, 3 * HD), data.dtype).at[slot_row].set(data)]
    all_gather x1, waiting for transfers between devices: 0.02 us -> 21.4 us  [on_device(): lax.all_gather(proj_rows, 'seq', axis=1, tiled=True)]
    all_to_all x1 -> x0, starting transfers between devices: 18.4 us -> none  [on_device(): lax.all_to_all(send_pos, 'seq', split_axis=1, concat_axis=1, tiled=True)]
    all_to_all x1, starting transfers between devices: 13.7 us -> 18.4 us  [on_device(): lax.all_to_all(send_rows, 'seq', split_axis=1, concat_axis=1, tiled=True)]
    gather x1 -> x0, local copies, waits for them, and re-layouts: 3.18 us -> none  [on_device(): picked = jnp.take_along_axis(returned, slot_index[:, :, None], axis=1)]
    reduce_scatter x1, waiting for transfers between devices: 28.4 us -> 31.4 us  [on_device(): lax.psum_scatter(rounded, 'head', scatter_dimension=1, tiled=True)]
  transfers between devices with their start and end apart: 6 -> 5, of which waited for: 3 -> 4; matrix products, arithmetic and copies ran while one was open for 37% -> 14% of each run, Pallas kernels for 0% -> 0%
where the time goes in v1:
time: 168 us; the launch traced here: 167 us
  waiting for transfers between devices  86.7 us (52%)
  starting transfers between devices  35.3 us (21%)
  matrix products  15.9 us (9%)
  between operations  13.6 us (8%)
  local copies, waits for them, and re-layouts  8.9 us (5%)
  other arithmetic  6.95 us (4%)
    reduce_scatter x1, waiting for transfers between devices, on_device(): lax.psum_scatter(rounded, 'head', scatter_dimension=1, tiled=True)  31.4 us
    ppermute x1, waiting for transfers between devices, shifted(): return lax.ppermute(block, axis, route)  21.5 us
    all_gather x1, waiting for transfers between devices, on_device(): lax.all_gather(proj_rows, 'seq', axis=1, tiled=True)  21.4 us
    all_to_all x1, starting transfers between devices, on_device(): lax.all_to_all(send_rows, 'seq', split_axis=1, concat_axis=1, tiled=True)  18.4 us
    all_to_all x1, starting transfers between devices, on_device(): lax.all_to_all(answered, 'seq', split_axis=1, concat_axis=1, tiled=True)  13.2 us
    all_to_all x1, waiting for transfers between devices, on_device(): lax.all_to_all(answered, 'seq', split_axis=1, concat_axis=1, tiled=True)  12.4 us
    dot_general x1, matrix products, on_device(): jnp.dot(joined, lax.all_gather(proj_rows, 'seq', axis=1, tiled=True), pre...  7.2 us
    dot_general x2, matrix products, attend(): jnp.einsum('...qd,...kd->...qk', query, keys, preferred_element_type=jnp....  3.62 us
  transfers between devices with their start and end apart: 5, of which 4 were waited for; matrix products, arithmetic and copies ran while one was open for 14% of the time, Pallas kernels for 0%

profile of v1, /device:TPU:1, one launch (start us, length us, event | category | flops | bytes accessed | tf_op | source)
XLA Modules:
  0.0 167.3 jit_solution(8494341244411517680)
XLA Ops:
  6.5 1.4 pad_maximum_fusion
  8.0 0.7 copy.70
  8.7 1.3 copy.45
  10.0 0.2 convert_reduce_fusion.1
  10.3 0.7 multiply_add_fusion
  10.9 0.2 convert_reduce_fusion
  11.2 0.4 add_convert_fusion
  11.6 1.7 %copy.48 = bf16[2,512,384]{2,0,1:T(2,128)(2,1)} copy(bf16[2,512,384]{2,1,0:T(8,128)(2,1)S(1)} %add_convert_fusion) | data formatting | bytes 1572864 | tf_op jit(solution)/shard_map/convert_element_type | solution.py:59
  13.3 18.4 %all-to-all-start = ((bf16[2,512,384]{2,0,1:T(2,128)(2,1)}), bf16[2,512,384]{2,0,1:T(2,128)(2,1)S(1)}, u32[]{:S(2)}, u32[]{:S(2)}) async-start(bf16[2,512,384]{2,0,1:T(2,128)(2,1)} %copy.48), calls=%async_computation | async-start | bytes 1572864 | tf_op jit(solution)/shard_map/all_to_all | solution.py:60
  31.8 0.6 copy.54
  32.4 0.7 copy.55
  33.2 3.5 %collective-permute-start = (bf16[2,6,256,128]{3,2,1,0:T(8,128)(2,1)S(1)}, bf16[2,6,256,128]{3,2,1,0:T(8,128)(2,1)S(1)}, u32[]{:S(2)}, u32[]{:S(2)}) collective-permute-start(bf16[2,6,256,128]{3,2,1,0:T(8,128)(2,1)S(1)} %stack.4), channel_id=1, source_target_pairs={{0,4},{4,8},{8,12},{12,16},{16,20},{20,24},{24,28},{28,32},{32,36}... | collective-permute-start | bytes 2359304 | tf_op jit(solution)/shard_map/ppermute | solution.py:17
  36.8 0.6 iota_compare_fusion.3
  37.4 0.9 compare_and_fusion
  38.3 0.8 slice_bitcast_fusion
  39.1 21.5 %collective-permute-done = bf16[2,6,256,128]{3,2,1,0:T(8,128)(2,1)S(1)} collective-permute-done((bf16[2,6,256,128]{3,2,1,0:T(8,128)(2,1)S(1)}, bf16[2,6,256,128]{3,2,1,0:T(8,128)(2,1)S(1)}, u32[]{:S(2)}, u32[]{:S(2)}) %collective-permute-start) | collective-permute-done | bytes 786464 | tf_op jit(solution)/shard_map/ppermute | solution.py:17
  60.6 0.8 slice_bitcast_fusion.1
  61.4 2.3 %fusion.12 = f32[6,512,256]{2,1,0:T(8,128)} fusion(bf16[6,256,128]{2,1,0:T(8,128)(2,1)S(1)} %get-tuple-element.6, bf16[6,256,128]{2,1,0:T(8,128)(2,1)S(1)} %get-tuple-element.8, bf16[3,6,256,128]{3,2,1,0:T(8,128)(2,1)S(1)} %bitcast.52), kind=kOutput, calls=%fused_computation.23 | convolution fusion | flops 202899456 | bytes 4325376 | tf_op jit(solution)/shard_map/...qd,...kd->...qk/dot_general | solution.py:21
  63.8 0.6 copy.69
  64.4 0.3 reshape.169
  64.9 0.6 fusion.41
  65.6 1.3 fusion.9
  66.9 2.2 %convolution_convert_fusion.1 = bf16[2,2,256,128]{3,2,1,0:T(8,128)(2,1)S(1)} fusion(f32[2,2,256]{2,1,0:T(2,128)S(1)} %fusion.41, bf16[2,2,256,384]{3,2,1,0:T(8,128)(2,1)} %copy-done.1, f32[2,2,256,256]{2,3,1,0:T(8,128)} %fusion.9), kind=kOutput, calls=%fused_computation.17 | convolution fusion | flops 68027648 | bytes 2625536 | tf_op jit(solution)/shard_map/...qk,...kd->...qd/dot_general | solution.py:28
  69.3 1.0 copy.52
  70.3 13.2 %all-to-all-start.1 = ((bf16[2,512,128]{2,0,1:T(2,128)(2,1)}), bf16[2,512,128]{2,0,1:T(2,128)(2,1)}, u32[]{:S(2)}, u32[]{:S(2)}) async-start(bf16[2,512,128]{2,0,1:T(2,128)(2,1)} %copy.52), calls=%async_computation.1 | async-start | bytes 524288 | tf_op jit(solution)/shard_map/all_to_all | solution.py:78
  83.7 2.6 %fusion.40 = (f32[6,256]{1,0:T(8,128)S(1)}, f32[6,256,512]{1,2,0:T(8,128)S(1)}) fusion(f32[6,512,256]{2,1,0:T(8,128)S(1)} %copy-done, pred[256,512]{0,1:T(8,128)(4,1)} %compare_and_fusion), kind=kOutput, calls=%fused_computation.66 | output fusion | flops 4719103 | bytes 6428672 | tf_op jit(solution)/shard_map/sub | solution.py:26
  86.3 0.5 fusion.10
  86.8 12.4 %all-to-all-done.1 = bf16[2,512,128]{2,0,1:T(2,128)(2,1)} async-done(((bf16[2,512,128]{2,0,1:T(2,128)(2,1)}), bf16[2,512,128]{2,0,1:T(2,128)(2,1)}, u32[]{:S(2)}, u32[]{:S(2)}) %all-to-all-start.1) | async-done | bytes 262176 | tf_op jit(solution)/shard_map/all_to_all | solution.py:78
  99.2 1.3 convolution_convert_fusion.2
  100.5 21.4 %all-gather.2.cloned.1.call-done = bf16[1024,4096]{0,1:T(8,128)(2,1)} async-done(((bf16[1024,32]{0,1:T(8,128)(2,1)}), bf16[1024,4096]{0,1:T(8,128)(2,1)}) %all-gather.2.cloned.1.call-update) | async-done | bytes 8388624 | tf_op jit(solution)/shard_map/all_gather | solution.py:100
  121.9 7.2 %convolution_convert_fusion = bf16[256,4096]{1,0:T(8,128)(2,1)} fusion(bf16[1024,4096]{0,1:T(8,128)(2,1)} %all-gather.2.cloned.1.call-done, bf16[256,768]{0,1:T(8,128)(2,1)S(1)} %bitcast.61, bf16[256,256]{0,1:T(8,128)(2,1)S(1)} %bitcast.62), kind=kOutput, calls=%fused_computation.2 | convolution fusion | flops 2149580800 | bytes 11010048 | tf_op jit(solution)/shard_map/dot_general | solution.py:98
  129.2 31.4 %reduce-scatter.2.cloned.1.call-done = bf16[256,1024]{1,0:T(8,128)(2,1)} async-done(((bf16[256,4096]{1,0:T(8,128)(2,1)}), bf16[256,1024]{1,0:T(8,128)(2,1)}) %reduce-scatter.2.cloned.1.call-update) | async-done | bytes 524304 | tf_op jit(solution)/shard_map/reduce_scatter | solution.py:105
  (26 shorter events, 0.9 us)
Async XLA Ops:
  6.5 115.4 %all-gather.2.cloned.1.call-start = ((), (), s32[]{:S(2)}) async-start(), calls=%async_computation.3 | async-start | bytes 8454144 | tf_op jit(solution)/shard_map/all_gather | solution.py:100
  8.7 23.1 %copy-start.2 = (bf16[3,256,768]{2,1,0:T(8,128)(2,1)S(1)}, bf16[3,256,768]{2,1,0:T(8,128)(2,1)}, u32[]{:S(2)}) copy-start(bf16[3,256,768]{2,1,0:T(8,128)(2,1)} %param.6) | copy-start | bytes 3538948
  13.3 50.4 %all-to-all-start = ((bf16[2,512,384]{2,0,1:T(2,128)(2,1)}), bf16[2,512,384]{2,0,1:T(2,128)(2,1)S(1)}, u32[]{:S(2)}, u32[]{:S(2)}) async-start(bf16[2,512,384]{2,0,1:T(2,128)(2,1)} %copy.48), calls=%async_computation | async-start | bytes 1572864 | tf_op jit(solution)/shard_map/all_to_all | solution.py:60
  33.2 27.4 %collective-permute-start = (bf16[2,6,256,128]{3,2,1,0:T(8,128)(2,1)S(1)}, bf16[2,6,256,128]{3,2,1,0:T(8,128)(2,1)S(1)}, u32[]{:S(2)}, u32[]{:S(2)}) collective-permute-start(bf16[2,6,256,128]{3,2,1,0:T(8,128)(2,1)S(1)} %stack.4), channel_id=1, source_target_pairs={{0,4},{4,8},{8,12},{12,16},{16,20},{20,24},{24,28},{28,32},{32,36}... | collective-permute-start | bytes 2359304 | tf_op jit(solution)/shard_map/ppermute | solution.py:17
  61.4 3.5 %copy-start.5 = (pred[256,256]{0,1:T(8,128)(4,1)S(1)}, pred[256,256]{0,1:T(8,128)(4,1)}, u32[]{:S(2)}) copy-start(pred[256,256]{0,1:T(8,128)(4,1)} %iota_compare_fusion.3) | copy-start | bytes 196612
  64.7 0.9 copy-start.1
  66.9 16.8 %copy-start = (f32[6,512,256]{2,1,0:T(8,128)S(1)}, f32[6,512,256]{2,1,0:T(8,128)}, u32[]{:S(2)}) copy-start(f32[6,512,256]{2,1,0:T(8,128)} %fusion.12) | copy-start | bytes 9437188
  70.3 28.9 %all-to-all-start.1 = ((bf16[2,512,128]{2,0,1:T(2,128)(2,1)}), bf16[2,512,128]{2,0,1:T(2,128)(2,1)}, u32[]{:S(2)}, u32[]{:S(2)}) async-start(bf16[2,512,128]{2,0,1:T(2,128)(2,1)} %copy.52), calls=%async_computation.1 | async-start | bytes 524288 | tf_op jit(solution)/shard_map/all_to_all | solution.py:78
  83.5 2.9 %copy-start.3 = (bf16[6,256,128]{2,1,0:T(8,128)(2,1)S(1)}, bf16[6,256,128]{2,1,0:T(8,128)(2,1)}, u32[]{:S(2)}) copy-start(bf16[6,256,128]{2,1,0:T(8,128)(2,1)} %get-tuple-element.5) | copy-start | bytes 1179652
  83.5 77.0 %reduce-scatter.2.cloned.1.call-start = ((), (), s32[]{:S(2)}) async-start(), calls=%async_computation.4 | async-start | bytes 2621440 | tf_op jit(solution)/shard_map/reduce_scatter | solution.py:105
  83.7 2.6 %copy-start.4 = (bf16[6,256,128]{2,1,0:T(8,128)(2,1)S(1)}, bf16[6,256,128]{2,1,0:T(8,128)(2,1)}, u32[]{:S(2)}) copy-start(bf16[6,256,128]{2,1,0:T(8,128)(2,1)} %get-tuple-element.7) | copy-start | bytes 1179652
Sparse Core Ops, SparseCore 0:
  10.5 111.3 all-gather.1
  129.3 31.1 reduce-scatter.1

commit v2 on v1

v2 whole, which is shorter than its diff:
```python
import functools
import math

import jax
import jax.numpy as jnp
from jax import lax
from jax.experimental import pallas as pl
from jax.experimental.pallas import tpu as pltpu
from jax.sharding import PartitionSpec as P

HD = 128
TOK = 256
LOCAL = 6
SIDE = 8
GROUPS = 4
EMPTY = 128.0
NEVER = -1e30
SCALE = 1.0 / math.sqrt(HD)
BF = jnp.bfloat16
F32 = jnp.float32
I32 = jnp.int32
NT = (((1,), (1,)), ((), ()))
NN = (((1,), (0,)), ((), ()))
TN = (((0,), (0,)), ((), ()))


def dot(a, b, dims):
    return lax.dot_general(a, b, dims, preferred_element_type=F32)


def iota(shape, axis):
    return lax.broadcasted_iota(I32, shape, axis)


def div(a, b):
    return lax.div(a, jnp.int32(b))


def rem(a, b):
    return lax.rem(a, jnp.int32(b))


def kernel(
    routed, local, code, wr, wl, out,
    own_x, own_code, place, sent, via, got, answer, back, final, picked, routed_out, acts, halo,
    turned_w, wt, stage_a, stage_b, arrived,
    a0_s, a0_r, halo_s, halo_r, wx_s, wx_r, p1_s, p1_r, p2_s, p2_r, w1_s, w1_r,
    ring_s, ring_r, sib_s, sib_r, q1_s, q1_r, q2_s, q2_r, ax_s, ax_r, xa_s, xa_r, xb_s, xb_r,
):
    h = lax.axis_index("head")
    s = lax.axis_index("seq")
    c = rem(s, 2)
    oc = 1 - c
    chip = div(s, 2)
    z = rem(chip, SIDE)
    y = div(chip, SIDE)
    u = z * oc + y * c
    w = y * oc + z * c
    sibling = s + 1 - 2 * c

    def seq_yz(yy, zz):
        return (yy * SIDE + zz) * 2 + c

    def seq_uw(uu, ww):
        return seq_yz(ww * oc + uu * c, uu * oc + ww * c)

    def to_seq(src, dst, ss, rs, seq):
        return pltpu.make_async_remote_copy(
            src_ref=src, dst_ref=dst, send_sem=ss, recv_sem=rs,
            device_id={"seq": seq}, device_id_type=pl.DeviceIdType.MESH,
        )

    def to_head(src, dst, ss, rs, head):
        return pltpu.make_async_remote_copy(
            src_ref=src, dst_ref=dst, send_sem=ss, recv_sem=rs,
            device_id={"head": head}, device_id_type=pl.DeviceIdType.MESH,
        )

    barrier = pltpu.get_barrier_semaphore()
    for j in range(1, SIDE):
        for target in (seq_uw(rem(u + j, SIDE), w), seq_uw(u, rem(w + j, SIDE))):
            pl.semaphore_signal(barrier, inc=1, device_id={"seq": target}, device_id_type=pl.DeviceIdType.MESH)
    pl.semaphore_signal(barrier, inc=1, device_id={"seq": sibling}, device_id_type=pl.DeviceIdType.MESH)
    for j in range(1, GROUPS):
        pl.semaphore_signal(
            barrier, inc=1, device_id={"head": rem(h + j, GROUPS)}, device_id_type=pl.DeviceIdType.MESH
        )

    @pl.when((c == 0) & (s > 0))
    def _():
        pl.semaphore_signal(barrier, inc=1, device_id={"seq": s - 1}, device_id_type=pl.DeviceIdType.MESH)

    pl.semaphore_wait(barrier, 2 * (SIDE - 1) + 1 + GROUPS - 1 + c * (1 - div(s, 2 * SIDE * SIDE - 1)))

    a0 = [
        to_seq(
            routed.at[j, :, pl.ds(pl.multiple_of(oc * HD, HD), HD)],
            own_x.at[c, :, pl.ds(j * HD, HD)],
            a0_s.at[j], a0_r.at[j], sibling,
        )
        for j in range(3)
    ]
    a0.append(to_seq(code.at[oc], own_code.at[c], a0_s.at[3], a0_r.at[3], sibling))
    for copy in a0:
        copy.start()
    halo_copy = to_seq(local.at[pl.ds(1, 2)], halo, halo_s, halo_r, s + 1)

    @pl.when(s < 2 * SIDE * SIDE - 1)
    def _():
        halo_copy.start()

    for core in range(2):

        @pl.when(c == core)
        def _():
            for j in range(3):
                own_x[core, :, j * HD : (j + 1) * HD] = routed[j, :, core * HD : (core + 1) * HD]
            own_code[core] = code[core]

    def block_of(yy, zz):
        return wt.at[
            div(yy, 2), rem(yy, 2), div(zz, 4), rem(div(zz, 2), 2),
            pl.ds(pl.multiple_of(rem(zz, 2) * 64, 64), 64),
        ]

    def part_of(core):
        return wt.at[
            div(y, 2), rem(y, 2), div(z, 4), rem(div(z, 2), 2),
            pl.ds(pl.multiple_of(rem(z, 2) * 64 + core * 32, 32), 32),
        ]

    def holder(yy, zz):
        return rem(yy + div(zz, 2), 2)

    eye = (iota((32, 32), 0) == iota((32, 32), 1)).astype(F32).astype(BF)
    own_rows = jnp.concatenate([dot(eye, wr[...], NT), dot(eye, wl[...], NT)], axis=1).astype(BF)
    holds = holder(y, z) == c
    wx_send = to_seq(turned_w, part_of(c), wx_s, wx_r, sibling)
    wx_recv = to_seq(turned_w, part_of(oc), wx_s, wx_r, sibling)

    @pl.when(holds)
    def _():
        part_of(c)[...] = own_rows

    @pl.when(jnp.logical_not(holds))
    def _():
        turned_w[...] = own_rows
        wx_send.start()

    for j in range(3):
        to_seq(
            routed.at[j, :, pl.ds(pl.multiple_of(oc * HD, HD), HD)],
            own_x.at[oc, :, pl.ds(j * HD, HD)],
            a0_s.at[j], a0_r.at[j], sibling,
        ).wait_recv()
    to_seq(code.at[oc], own_code.at[oc], a0_s.at[3], a0_r.at[3], sibling).wait_recv()

    def rows_of(b):
        value = own_code[b]
        rank = value & 1
        cluster = value >> 1
        owner = cluster >> 2
        turned = (owner & 7) * SIDE + (owner >> 3)
        goes = turned * oc + owner * c
        return goes * 16 + b * 8 + (cluster & 3) * 2 + rank

    slot = jnp.concatenate([rows_of(0), rows_of(1)], axis=1)[0:1]
    both = own_x[...].reshape(2 * TOK, 3 * HD)
    ones = jnp.ones((2 * TOK, HD), BF)
    for i in range(4):
        hot = (iota((256, 2 * TOK), 0) + i * 256 == slot).astype(F32).astype(BF)
        place[i * 256 : (i + 1) * 256] = hot
        rows = dot(hot, both, NN)
        filled = dot(hot, ones, NN)
        lead = (1.0 - filled) * EMPTY
        rows = jnp.concatenate([rows[:, :HD], rows[:, HD : 2 * HD] + lead, rows[:, 2 * HD :]], axis=1)
        sent[2 * i : 2 * i + 2] = rows.astype(BF).reshape(2, SIDE, 16, 3 * HD)

    def p1(j, sending):
        there, here = rem(u + j, SIDE), rem(u + SIDE - j, SIDE)
        dst = via.at[u] if sending else via.at[here]
        return to_seq(sent.at[there], dst, p1_s.at[j], p1_r.at[j], seq_uw(there, w))

    for j in range(1, SIDE):
        p1(j, True).start()
    via[u] = sent[u]

    def w1(j, core, sending):
        if core == 0:
            target = seq_yz(y, rem(z + j, SIDE))
            blk = block_of(y, z) if sending else block_of(y, rem(z + SIDE - j, SIDE))
        else:
            target = seq_yz(rem(y + j, SIDE), z)
            blk = block_of(y, z) if sending else block_of(rem(y + SIDE - j, SIDE), z)
        return to_seq(blk, blk, w1_s.at[j], w1_r.at[j], target)

    @pl.when(holds)
    def _():
        wx_recv.wait_recv()
        for core in range(2):

            @pl.when(c == core)
            def _():
                for j in range(1, SIDE):
                    w1(j, core, True).start()

    for j in range(1, SIDE):
        p1(j, False).wait_recv()

    def p2(j, sending):
        there, here = rem(w + j, SIDE), rem(w + SIDE - j, SIDE)
        dst = got.at[w] if sending else got.at[here]
        return to_seq(via.at[:, there], dst, p2_s.at[j], p2_r.at[j], seq_uw(u, there))

    for j in range(1, SIDE):
        p2(j, True).start()
    for i in range(SIDE):
        got[w, i] = via[i, w]

    for core in range(2):

        @pl.when(c == core)
        def _():
            for j in range(1, SIDE):
                if core == 0:
                    is_source = holder(y, rem(z + SIDE - j, SIDE)) == 0
                else:
                    is_source = holder(rem(y + SIDE - j, SIDE), z) == 1

                @pl.when(is_source)
                def _():
                    w1(j, core, False).wait_recv()

    def blocks(core, place_on):
        at = rem(place_on + SIDE, SIDE)
        if core == 0:
            return wt.at[div(at, 2), rem(at, 2), :, rem(at, 2)]
        par = rem(div(at, 2), 2)
        return wt.at[:, 1 - par, div(at, 4), par, pl.ds(pl.multiple_of(rem(at, 2) * 64, 64), 64)]

    def half(ref, k, way):
        return ref.at[:, :, pl.ds(way * 512, 512)] if k == SIDE // 2 else ref

    def ring(k, way, core, sending):
        coord = y if core == 0 else z
        sign = 1 - 2 * way
        if sending:
            blk = blocks(core, coord - sign * (k - 1))
        else:
            blk = blocks(core, coord - sign * k)
        blk = half(blk, k, way)
        to = rem(coord + sign + SIDE, SIDE)
        target = seq_yz(to, z) if core == 0 else seq_yz(y, to)
        return to_seq(blk, blk, ring_s.at[k, way], ring_r.at[k, way], target)

    def sib(k, way, path):
        coord = y if path == 0 else z
        blk = blocks(path, coord - (1 - 2 * way) * k)
        return to_seq(blk, blk, sib_s.at[k, way], sib_r.at[k, way], sibling)

    def ways(k):
        return (0,) if k in (0, SIDE // 2) else (0, 1)

    def by_core(body):
        for core in range(2):
            pl.when(c == core)(functools.partial(body, core))

    def ring_step(k):
        def body(core):
            if k > 1:
                for way in range(2):
                    ring(k - 1, way, core, False).wait_recv()
            if k <= SIDE // 2:
                for way in range(2):
                    ring(k, way, core, True).start()
            for way in ways(k - 1):
                sib(k - 1, way, core).start()

        by_core(body)

    def sib_wait(k):
        def body(core):
            for way in ways(k):
                sib(k, way, 1 - core).wait_recv()

        by_core(body)

    ring_step(1)

    @pl.when(s > 0)
    def _():
        halo_copy.wait_recv()

    @pl.when(s == 0)
    def _():
        halo[...] = jnp.zeros_like(halo)

    own_side = iota((TOK, TOK), 1) <= iota((TOK, TOK), 0)
    shift = jnp.where(s > 0, jnp.float32(0.0), jnp.float32(NEVER))
    for n in range(LOCAL):
        cols = slice(n * HD, (n + 1) * HD)
        query = local[0, :, cols]
        here = dot(query, local[1, :, cols], NT) * SCALE
        before = dot(query, halo[0, :, cols], NT) * SCALE + shift
        scores = jnp.where(own_side, here, before)
        raised = jnp.exp(scores - jnp.max(scores, axis=1, keepdims=True))
        weights = raised / jnp.sum(raised, axis=1, keepdims=True)
        near = jnp.where(own_side, weights, 0.0).astype(BF)
        far = jnp.where(own_side, 0.0, weights).astype(BF)
        result = dot(near, local[2, :, cols], NN) + dot(far, halo[1, :, cols], NN)
        acts[:, (2 + n) * HD : (3 + n) * HD] = result.astype(BF)

    for j in range(1, SIDE):
        p2(j, False).wait_recv()

    def code_of(r):
        first, second = (r >> 7) & 7, (r >> 4) & 7
        place_of = (first * SIDE + second) * oc + (second * SIDE + first) * c
        return ((r >> 1) & 3) * 4096 + place_of * 4 + ((r >> 3) & 1) * 2 + (r & 1)

    keys = got[:, :, :, HD : 2 * HD].reshape(1024, HD)
    values = got[:, :, :, 2 * HD :].reshape(1024, HD)
    lane_zero = (iota((8, HD), 1) == 0).astype(F32).astype(BF)
    lead_key = dot(lane_zero, keys, NT)[0:1]
    key_code = jnp.where(lead_key < 0.75 * EMPTY, code_of(iota((8, 1024), 1))[0:1], 1 << 20)
    for i in range(4):
        query = got[2 * i : 2 * i + 2, :, :, 0:HD].reshape(256, HD)
        scores = dot(query, keys, NT) * SCALE
        ahead = code_of(iota((256, HD), 0) + i * 256)[:, 0:1] - key_code
        scores = jnp.where((ahead >= 0) & (ahead < 256), scores, NEVER)
        raised = jnp.exp(scores - jnp.max(scores, axis=1, keepdims=True))
        weights = (raised / jnp.sum(raised, axis=1, keepdims=True)).astype(BF)
        answer[2 * i : 2 * i + 2] = dot(weights, values, NN).astype(BF).reshape(2, SIDE, 16, HD)

    def q1(j, sending):
        there, here = rem(w + j, SIDE), rem(w + SIDE - j, SIDE)
        dst = back.at[w] if sending else back.at[here]
        return to_seq(answer.at[there], dst, q1_s.at[j], q1_r.at[j], seq_uw(u, there))

    for j in range(1, SIDE):
        q1(j, True).start()
    back[w] = answer[w]

    ring_step(2)

    for j in range(1, SIDE):
        q1(j, False).wait_recv()

    def q2(j, sending):
        there, here = rem(u + j, SIDE), rem(u + SIDE - j, SIDE)
        dst = final.at[u] if sending else final.at[here]
        return to_seq(back.at[:, there], dst, q2_s.at[j], q2_r.at[j], seq_uw(there, w))

    for j in range(1, SIDE):
        q2(j, True).start()
    for i in range(SIDE):
        final[u, i] = back[i, u]

    ring_step(3)

    for j in range(1, SIDE):
        q2(j, False).wait_recv()
    tokens = dot(place[...], final[...].reshape(1024, HD), TN).astype(BF)
    picked[0] = tokens[:TOK]
    picked[1] = tokens[TOK:]
    ax_send = to_seq(picked.at[oc], routed_out.at[c], ax_s, ax_r, sibling)
    ax_send.start()
    routed_out[c] = picked[c]
    to_seq(picked.at[oc], routed_out.at[oc], ax_s, ax_r, sibling).wait_recv()
    acts[:, 0:HD] = routed_out[0]
    acts[:, HD : 2 * HD] = routed_out[1]

    def send_a(yy):
        head, e = div(yy, 2), rem(yy, 2)
        return to_head(
            stage_a.at[yy], arrived.at[h, e, :, e], xa_s.at[yy],
            xa_r.at[rem(head + GROUPS - h, GROUPS), e], head,
        )

    def send_b(pair, head):
        q, par = div(pair, 2), rem(pair, 2)
        return to_head(
            stage_b.at[pair, head], arrived.at[h, 1 - par, q, par], xb_s.at[pair, head],
            xb_r.at[rem(head + GROUPS - h, GROUPS), pair], jnp.int32(head),
        )

    def project_a(at):
        yy = rem(at + SIDE, SIDE)
        head, e = div(yy, 2), rem(yy, 2)
        rows = jnp.concatenate([wt[head, e, 0, e], wt[head, e, 1, e]], axis=0)
        share = dot(acts[...], rows, NT).astype(BF)
        stage_a[yy, 0] = share[:, :HD]
        stage_a[yy, 1] = share[:, HD:]

        @pl.when(head == h)
        def _():
            arrived[h, e, 0, e] = share[:, :HD]
            arrived[h, e, 1, e] = share[:, HD:]

        @pl.when(head != h)
        def _():
            send_a(yy).start()

    def project_b(at):
        pair = rem(at + 4, 4)
        q, par = div(pair, 2), rem(pair, 2)
        rows = jnp.concatenate([wt[i, 1 - par, q, par] for i in range(4)], axis=0)
        share = dot(acts[...], rows, NT).astype(BF)
        for head in range(GROUPS):
            tile = share[:, head * HD : (head + 1) * HD]
            stage_b[pair, head] = tile

            @pl.when(h == head)
            def _():
                arrived[h, 1 - par, q, par] = tile

            @pl.when(h != head)
            def _():
                send_b(pair, head).start()

    zb, zp = rem(z, 2), div(z, 2)
    turn = 1 - 2 * zb
    sib_wait(0)
    project_a(y)
    sib_wait(1)
    project_b(zp)
    project_a(y - 1)
    project_a(y + 1)
    sib_wait(2)
    project_b(zp - turn + 4)
    project_a(y - 2)
    project_a(y + 2)
    ring_step(4)
    sib_wait(3)
    project_b(zp + turn)
    project_a(y - 3)
    project_a(y + 3)
    ring_step(5)
    sib_wait(4)
    project_b(zp + 2)
    project_a(y + 4)

    for j in range(1, GROUPS):
        src = rem(h + GROUPS - j, GROUPS)
        for e in range(2):
            to_head(
                stage_a.at[0], arrived.at[src, e, :, e], xa_s.at[0], xa_r.at[j, e], src
            ).wait_recv()
        for pair in range(4):
            q, par = pair // 2, pair % 2
            to_head(
                stage_b.at[0, 0], arrived.at[src, 1 - par, q, par], xb_s.at[0, 0], xb_r.at[j, pair], src
            ).wait_recv()
    for e in range(2):
        for q in range(2):
            for par in range(2):
                total = arrived[0, e, q, par].astype(F32)
                for g in range(1, GROUPS):
                    total = total + arrived[g, e, q, par].astype(F32)
                first = e * 512 + (2 * q + par) * HD
                out[:, first : first + HD] = total.astype(BF)

    for copy in a0:
        copy.wait_send()

    @pl.when(s < 2 * SIDE * SIDE - 1)
    def _():
        halo_copy.wait_send()

    @pl.when(jnp.logical_not(holds))
    def _():
        wx_send.wait_send()

    for j in range(1, SIDE):
        for stage in (p1, p2, q1, q2):
            stage(j, True).wait_send()

    def drain(core):
        @pl.when(holds)
        def _():
            for j in range(1, SIDE):
                w1(j, core, True).wait_send()

        for k in range(1, SIDE // 2 + 1):
            for way in range(2):
                ring(k, way, core, True).wait_send()
        for k in range(SIDE // 2 + 1):
            for way in ways(k):
                sib(k, way, core).wait_send()

    by_core(drain)
    ax_send.wait_send()
    for yy in range(SIDE):

        @pl.when(h != yy // 2)
        def _():
            send_a(jnp.int32(yy)).wait_send()

    for head in range(GROUPS):

        @pl.when(h != head)
        def _():
            for pair in range(4):
                send_b(jnp.int32(pair), head).wait_send()


def on_device(routed_qkv, local_qkv, cluster_ids, wo_routed, wo_local):
    cluster = cluster_ids[:, :, 0]
    order = jnp.arange(TOK, dtype=I32)
    same = (cluster[:, :, None] == cluster[:, None, :]) & (order[None, :, None] < order[None, None, :])
    rank = jnp.sum(same.astype(I32), axis=1)
    code = jnp.broadcast_to((cluster * 2 + rank)[:, None, :], (2, 8, TOK))
    sems = [
        (4,), (4,), (), (), (), (), (8,), (8,), (8,), (8,), (8,), (8,),
        (5, 2), (5, 2), (5, 2), (5, 2), (8,), (8,), (8,), (8,), (), (),
        (8,), (4, 2), (4, 4), (4, 4),
    ]
    scratch = [
        pltpu.VMEM((2, TOK, 3 * HD), BF),
        pltpu.VMEM((2, 8, TOK), I32),
        pltpu.VMEM((1024, 2 * TOK), BF),
        pltpu.VMEM((8, 8, 16, 3 * HD), BF),
        pltpu.VMEM((8, 8, 16, 3 * HD), BF),
        pltpu.VMEM((8, 8, 16, 3 * HD), BF),
        pltpu.VMEM((8, 8, 16, HD), BF),
        pltpu.VMEM((8, 8, 16, HD), BF),
        pltpu.VMEM((8, 8, 16, HD), BF),
        pltpu.VMEM((2, TOK, HD), BF),
        pltpu.VMEM((2, TOK, HD), BF),
        pltpu.VMEM((TOK, 8 * HD), BF),
        pltpu.VMEM((2, TOK, LOCAL * HD), BF),
        pltpu.VMEM((32, 8 * HD), BF),
        pltpu.VMEM((4, 2, 2, 2, 128, 8 * HD), BF),
        pltpu.VMEM((8, 2, TOK, HD), BF),
        pltpu.VMEM((4, 4, TOK, HD), BF),
        pltpu.VMEM((4, 2, 2, 2, TOK, HD), BF),
    ]
    scratch += [pltpu.SemaphoreType.DMA(shape) if shape else pltpu.SemaphoreType.DMA for shape in sems]
    return pl.pallas_call(
        kernel,
        out_shape=jax.ShapeDtypeStruct((TOK, 1024), BF),
        in_specs=[pl.BlockSpec(memory_space=pltpu.VMEM)] * 5,
        out_specs=pl.BlockSpec(memory_space=pltpu.VMEM),
        scratch_shapes=scratch,
        compiler_params=pltpu.CompilerParams(
            collective_id=0, has_side_effects=True, vmem_limit_bytes=50 * 2**20
        ),
        cost_estimate=pl.CostEstimate(flops=4 * 10**9, bytes_accessed=3 * 2**20, transcendentals=2 * 10**6),
    )(routed_qkv, local_qkv, code, wo_routed, wo_local)


def solution(mesh):
    placed = (
        P(None, "seq", "head"),
        P(None, "seq", "head"),
        P("head", "seq", None),
        P("head", "seq"),
        P("head", "seq"),
    )
    return jax.shard_map(
        on_device, mesh=mesh, in_specs=placed, out_specs=P("seq", "head"), check_vma=False
    )
```

time: 168 us -> 110 us (0.65)
  Pallas kernels: 0 us -> 103 us
  waiting for transfers between devices: 86.7 us -> 0 us
  starting transfers between devices: 35.3 us -> 0 us
  matrix products: 15.9 us -> 0 us
  between operations: 13.6 us -> 0.03 us
  other arithmetic: 6.95 us -> 0.87 us
  local copies, waits for them, and re-layouts: 8.9 us -> 5.54 us
    pallas_call x0 -> x1, Pallas kernels: none -> 103 us  [on_device(): pl.pallas_call(kernel, out_shape=jax.ShapeDtypeStruct((TOK, 1024), BF), i...]
    all_to_all x2 -> x0, starting transfers between devices: 31.6 us -> none  [the longest x1 18.4 us: on_device(): lax.all_to_all(send_rows, 'seq', split_axis=1, concat_axis=1, tiled=True)]
    reduce_scatter x1 -> x0, waiting for transfers between devices: 31.4 us -> none  [on_device(): lax.psum_scatter(rounded, 'head', scatter_dimension=1, tiled=True)]
    ppermute x1 -> x0, waiting for transfers between devices: 21.5 us -> none  [shifted(): return lax.ppermute(block, axis, route)]
    all_gather x1 -> x0, waiting for transfers between devices: 21.4 us -> none  [on_device(): lax.all_gather(proj_rows, 'seq', axis=1, tiled=True)]
    dot_general x7 -> x0, matrix products: 15.3 us -> none  [the longest x1 7.2 us: on_device(): jnp.dot(joined, lax.all_gather(proj_rows, 'seq', axis=1, tiled=True), pre...]
    all_to_all x2 -> x0, waiting for transfers between devices: 12.4 us -> none  [the longest x1 12.4 us: on_device(): lax.all_to_all(answered, 'seq', split_axis=1, concat_axis=1, tiled=True)]
    ppermute x1 -> x0, starting transfers between devices: 3.54 us -> none  [shifted(): return lax.ppermute(block, axis, route)]
  transfers between devices with their start and end apart: 5 -> 0, of which waited for: 4 -> 0; matrix products, arithmetic and copies ran while one was open for 14% -> 0% of each run, Pallas kernels for 0% -> 0%
where the time goes in v2:
time: 110 us; the launch traced here: 109 us
  Pallas kernels  103 us (94%)
  local copies, waits for them, and re-layouts  5.54 us (5%)
    pallas_call x1, Pallas kernels, on_device(): pl.pallas_call(kernel, out_shape=jax.ShapeDtypeStruct((TOK, 1024), BF), i...  103 us
    unnamed x8, local copies, waits for them, and re-layouts  5.54 us

profile of v2, /device:TPU:1, one launch (start us, length us, event | category | flops | bytes accessed | tf_op | source)
XLA Modules:
  0.0 109.0 jit_solution(2981424038065299860)
XLA Ops:
  0.0 0.7 copy.14
  0.7 0.8 copy.8.wr
  1.6 0.2 convert_reduce_fusion
  1.7 0.7 multiply_add_fusion
  2.4 1.0 copy.9.wl
  3.4 0.0 copy-start
  3.4 1.3 %copy-done = bf16[3,256,768]{2,1,0:T(8,128)(2,1)S(1)} copy-done((bf16[3,256,768]{2,1,0:T(8,128)(2,1)S(1)}, bf16[3,256,768]{2,1,0:T(8,128)(2,1)}, u32[]{:S(2)}) %copy-start) | copy-done | bytes 1179672
  4.6 0.0 copy-start.1
  4.6 1.0 copy-done.1
  5.6 102.6 %shard_map.55 = bf16[256,1024]{1,0:T(8,128)(2,1)S(1)} custom-call(bf16[3,256,256]{2,1,0:T(8,128)(2,1)S(1)} %copy-done.1, bf16[3,256,768]{2,1,0:T(8,128)(2,1)S(1)} %copy-done, s32[2,8,256]{2,1,0:T(8,128)S(1)} %broadcast_in_dim.2.code, bf16[256,32]{1,0:T(8,128)(2,1)S(1)} %copy.8.wr, bf16[768,32]{1,0:T(8,128)(2,1)S(1)} %copy.9.wl), custom_call_target="tpu_custom_call" | custom-call | flops 4000000000 | bytes 3145728 | tf_op jit(solution)/shard_map/pallas_call | solution.py:539
  108.2 0.8 copy.16
  (2 shorter events, 0.0 us)
Async XLA Ops:
  3.4 1.3 %copy-start = (bf16[3,256,768]{2,1,0:T(8,128)(2,1)S(1)}, bf16[3,256,768]{2,1,0:T(8,128)(2,1)}, u32[]{:S(2)}) copy-start(bf16[3,256,768]{2,1,0:T(8,128)(2,1)} %local.1) | copy-start | bytes 3538948
  4.6 1.0 copy-start.1

commit v3 on v2

v3 whole, which is shorter than its diff:
```python
import functools
import math

import jax
import jax.numpy as jnp
from jax import lax
from jax.experimental import pallas as pl
from jax.experimental.pallas import tpu as pltpu
from jax.sharding import PartitionSpec as P

HD = 128
TOK = 256
LOCAL = 6
SIDE = 8
GROUPS = 4
EMPTY = 128.0
NEVER = -1e30
SCALE = 1.0 / math.sqrt(HD)
BF = jnp.bfloat16
F32 = jnp.float32
I32 = jnp.int32
NT = (((1,), (1,)), ((), ()))
NN = (((1,), (0,)), ((), ()))
TN = (((0,), (0,)), ((), ()))


def dot(a, b, dims):
    return lax.dot_general(a, b, dims, preferred_element_type=F32)


def iota(shape, axis):
    return lax.broadcasted_iota(I32, shape, axis)


def each(low, high, body):
    def step(j, carry):
        body(j)
        return carry

    lax.fori_loop(low, high, step, jnp.int32(0))


def div(a, b):
    return lax.div(a, jnp.int32(b))


def rem(a, b):
    return lax.rem(a, jnp.int32(b))


def kernel(
    routed, local_in, ids, wr, wl, out,
    own_x, own_ids, local, place, sent, via, got, answer, back, final, picked, routed_out, acts, halo,
    wt, stage_a, stage_b, arrived,
    in_s, a0_s, a0_r, halo_s, halo_r, wx_s, wx_r, p1_s, p1_r, p2_s, p2_r, w1_s, w1_r,
    ring_s, ring_r, sib_s, sib_r, q1_s, q1_r, q2_s, q2_r, ax_s, ax_r, xa_s, xa_r, xb_s, xb_r,
):
    h = lax.axis_index("head")
    s = lax.axis_index("seq")
    c = rem(s, 2)
    oc = 1 - c
    chip = div(s, 2)
    z = rem(chip, SIDE)
    y = div(chip, SIDE)
    u = z * oc + y * c
    w = y * oc + z * c
    sibling = s + 1 - 2 * c

    def seq_yz(yy, zz):
        return (yy * SIDE + zz) * 2 + c

    def seq_uw(uu, ww):
        return seq_yz(ww * oc + uu * c, uu * oc + ww * c)

    def to_seq(src, dst, ss, rs, seq):
        return pltpu.make_async_remote_copy(
            src_ref=src, dst_ref=dst, send_sem=ss, recv_sem=rs,
            device_id={"seq": seq}, device_id_type=pl.DeviceIdType.MESH,
        )

    def to_head(src, dst, ss, rs, head):
        return pltpu.make_async_remote_copy(
            src_ref=src, dst_ref=dst, send_sem=ss, recv_sem=rs,
            device_id={"head": head}, device_id_type=pl.DeviceIdType.MESH,
        )

    barrier = pltpu.get_barrier_semaphore()

    def greet(j):
        for target in (seq_uw(rem(u + j, SIDE), w), seq_uw(u, rem(w + j, SIDE))):
            pl.semaphore_signal(barrier, inc=1, device_id={"seq": target}, device_id_type=pl.DeviceIdType.MESH)

    each(1, SIDE, greet)
    pl.semaphore_signal(barrier, inc=1, device_id={"seq": sibling}, device_id_type=pl.DeviceIdType.MESH)
    for j in range(1, GROUPS):
        pl.semaphore_signal(
            barrier, inc=1, device_id={"head": rem(h + j, GROUPS)}, device_id_type=pl.DeviceIdType.MESH
        )

    @pl.when((c == 0) & (s > 0))
    def _():
        pl.semaphore_signal(barrier, inc=1, device_id={"seq": s - 1}, device_id_type=pl.DeviceIdType.MESH)

    pl.semaphore_wait(barrier, 2 * (SIDE - 1) + 1 + GROUPS - 1 + c * (1 - div(s, 2 * SIDE * SIDE - 1)))

    def block_of(yy, zz):
        return wt.at[
            div(yy, 2), rem(yy, 2), div(zz, 4), rem(div(zz, 2), 2),
            pl.ds(pl.multiple_of(rem(zz, 2) * 64, 64), 64),
        ]

    def part_of(core, first, count):
        return wt.at[
            div(y, 2), rem(y, 2), div(z, 4), rem(div(z, 2), 2),
            pl.ds(pl.multiple_of(rem(z, 2) * 64 + core * 32, 32), 32), pl.ds(first, count),
        ]

    def holder(yy, zz):
        return rem(yy + div(zz, 2), 2)

    holds = holder(y, z) == c
    pieces = ((wr, 0, 2 * HD), (wl, 2 * HD, LOCAL * HD))
    w_keep = [
        pltpu.make_async_copy(ref, part_of(c, first, count), in_s.at[i])
        for i, (ref, first, count) in enumerate(pieces)
    ]
    w_send = [
        to_seq(ref, part_of(c, first, count), wx_s.at[i], wx_r.at[i], sibling)
        for i, (ref, first, count) in enumerate(pieces)
    ]
    w_take = [
        to_seq(ref, part_of(oc, first, count), wx_s.at[i], wx_r.at[i], sibling)
        for i, (ref, first, count) in enumerate(pieces)
    ]

    @pl.when(holds)
    def _():
        for copy in w_keep:
            copy.start()

    @pl.when(jnp.logical_not(holds))
    def _():
        for copy in w_send:
            copy.start()

    def head_rows(j, core):
        return routed.at[j, :, pl.ds(pl.multiple_of(core * HD, HD), HD)]

    def a0(core):
        copies = [
            to_seq(head_rows(j, oc), own_x.at[core, :, pl.ds(j * HD, HD)], a0_s.at[j], a0_r.at[j], sibling)
            for j in range(3)
        ]
        return copies + [to_seq(ids.at[oc], own_ids.at[core], a0_s.at[3], a0_r.at[3], sibling)]

    for copy in a0(c):
        copy.start()
    own = [
        pltpu.make_async_copy(head_rows(j, c), own_x.at[c, :, pl.ds(j * HD, HD)], in_s.at[2 + j])
        for j in range(3)
    ]
    own.append(pltpu.make_async_copy(ids.at[c], own_ids.at[c], in_s.at[5]))
    own.append(pltpu.make_async_copy(local_in, local, in_s.at[6]))
    for copy in own:
        copy.start()
    halo_copy = to_seq(local_in.at[pl.ds(1, 2)], halo, halo_s, halo_r, s + 1)
    own_x[:, :, 3 * HD :] = jnp.ones((2, TOK, HD), BF)

    def w1(j, core, sending):
        if core == 0:
            target = seq_yz(y, rem(z + j, SIDE))
            blk = block_of(y, z) if sending else block_of(y, rem(z + SIDE - j, SIDE))
        else:
            target = seq_yz(rem(y + j, SIDE), z)
            blk = block_of(y, z) if sending else block_of(rem(y + SIDE - j, SIDE), z)
        return to_seq(blk, blk, w1_s.at[j], w1_r.at[j], target)

    def by_core(body):
        for core in range(2):
            pl.when(c == core)(functools.partial(body, core))

    @pl.when(holds)
    def _():
        for copy in w_keep:
            copy.wait()
        for copy in w_take:
            copy.wait_recv()

        def send(core):
            each(1, SIDE, lambda j: w1(j, core, True).start())

        by_core(send)

    for copy in own[:4]:
        copy.wait()
    for copy in a0(oc):
        copy.wait_recv()

    def rows_of(b):
        cluster = own_ids[b]
        name = cluster.astype(F32)
        first_row = jnp.where(iota((8, TOK), 0) == 0, jnp.broadcast_to(name, (8, TOK)), 0.0).astype(BF)
        down = dot(first_row, jnp.ones((8, TOK), BF), TN)
        earlier = (down == name) & (iota((TOK, TOK), 0) < iota((TOK, TOK), 1))
        rank = jnp.sum(jnp.where(earlier, 1.0, 0.0), axis=0, keepdims=True).astype(I32)
        owner = cluster >> 2
        turned = (owner & 7) * SIDE + (owner >> 3)
        goes = turned * oc + owner * c
        return goes * 16 + b * 8 + (cluster & 3) * 2 + rank

    slot = jnp.concatenate([rows_of(0), rows_of(1)], axis=1)
    both = own_x[...].reshape(2 * TOK, 4 * HD)

    def fill(i):
        hot = (iota((256, 2 * TOK), 0) + i * 256 == slot).astype(F32).astype(BF)
        place[pl.ds(pl.multiple_of(i * 256, 256), 256)] = hot
        rows = dot(hot, both, NN)
        lead = (1.0 - rows[:, 3 * HD :]) * EMPTY
        rows = jnp.concatenate([rows[:, :HD], rows[:, HD : 2 * HD] + lead, rows[:, 2 * HD : 3 * HD]], axis=1)
        sent[pl.ds(2 * i, 2)] = rows.astype(BF).reshape(2, SIDE, 16, 3 * HD)

    each(0, 4, fill)

    def p1(j, sending):
        there, here = rem(u + j, SIDE), rem(u + SIDE - j, SIDE)
        dst = via.at[u] if sending else via.at[here]
        return to_seq(sent.at[there], dst, p1_s.at[j], p1_r.at[j], seq_uw(there, w))

    each(1, SIDE, lambda j: p1(j, True).start())
    via[u] = sent[u]

    @pl.when(s < 2 * SIDE * SIDE - 1)
    def _():
        halo_copy.start()

    for core in range(2):

        @pl.when(c == core)
        def _():
            def take(j):
                if core == 0:
                    is_source = holder(y, rem(z + SIDE - j, SIDE)) == 0
                else:
                    is_source = holder(rem(y + SIDE - j, SIDE), z) == 1

                @pl.when(is_source)
                def _():
                    w1(j, core, False).wait_recv()

            each(1, SIDE, take)

    def blocks(core, place_on):
        at = rem(place_on + SIDE, SIDE)
        if core == 0:
            return wt.at[div(at, 2), rem(at, 2), :, rem(at, 2)]
        par = rem(div(at, 2), 2)
        return wt.at[:, 1 - par, div(at, 4), par, pl.ds(pl.multiple_of(rem(at, 2) * 64, 64), 64)]

    def half(ref, k, way):
        return ref.at[:, :, pl.ds(way * 512, 512)] if k == SIDE // 2 else ref

    def ring(k, way, core, sending):
        coord = y if core == 0 else z
        sign = 1 - 2 * way
        if sending:
            blk = blocks(core, coord - sign * (k - 1))
        else:
            blk = blocks(core, coord - sign * k)
        blk = half(blk, k, way)
        to = rem(coord + sign + SIDE, SIDE)
        target = seq_yz(to, z) if core == 0 else seq_yz(y, to)
        return to_seq(blk, blk, ring_s.at[k, way], ring_r.at[k, way], target)

    def sib(k, way, path):
        coord = y if path == 0 else z
        blk = blocks(path, coord - (1 - 2 * way) * k)
        return to_seq(blk, blk, sib_s.at[k, way], sib_r.at[k, way], sibling)

    def ways(k):
        return (0,) if k in (0, SIDE // 2) else (0, 1)

    def ring_step(k):
        def body(core):
            if k > 1:
                for way in range(2):
                    ring(k - 1, way, core, False).wait_recv()
            if k <= SIDE // 2:
                for way in range(2):
                    ring(k, way, core, True).start()
            for way in ways(k - 1):
                sib(k - 1, way, core).start()

        by_core(body)

    def sib_wait(k):
        def body(core):
            for way in ways(k):
                sib(k, way, 1 - core).wait_recv()

        by_core(body)

    ring_step(1)

    each(1, SIDE, lambda j: p1(j, False).wait_recv())

    def p2(j, sending, core):
        there, here = rem(w + j, SIDE), rem(w + SIDE - j, SIDE)
        at = w if sending else here
        dst = got.at[at] if core == 0 else got.at[:, at]
        return to_seq(via.at[:, there], dst, p2_s.at[j], p2_r.at[j], seq_uw(u, there))

    def p2_start(core):
        each(1, SIDE, lambda j: p2(j, True, core).start())

        def keep(i):
            if core == 0:
                got[w, i] = via[i, w]
            else:
                got[i, w] = via[i, w]

        each(0, SIDE, keep)

    by_core(p2_start)

    own[4].wait()

    @pl.when(s > 0)
    def _():
        halo_copy.wait_recv()

    @pl.when(s == 0)
    def _():
        halo[...] = jnp.zeros_like(halo)

    own_side = iota((TOK, TOK), 1) <= iota((TOK, TOK), 0)
    shift = jnp.where(s > 0, jnp.float32(0.0), jnp.float32(NEVER))

    def window(n):
        cols = pl.ds(pl.multiple_of(n * HD, HD), HD)
        query = local[0, :, cols]
        here = dot(query, local[1, :, cols], NT) * SCALE
        before = dot(query, halo[0, :, cols], NT) * SCALE + shift
        scores = jnp.where(own_side, here, before)
        raised = jnp.exp(scores - jnp.max(scores, axis=1, keepdims=True))
        weights = raised * (1.0 / jnp.sum(raised, axis=1, keepdims=True))
        near = jnp.where(own_side, weights, 0.0).astype(BF)
        far = jnp.where(own_side, 0.0, weights).astype(BF)
        result = dot(near, local[2, :, cols], NN) + dot(far, halo[1, :, cols], NN)
        acts[:, pl.ds(pl.multiple_of((2 + n) * HD, HD), HD)] = result.astype(BF)

    each(0, LOCAL, window)

    ring_step(2)

    def p2_take(core):
        each(1, SIDE, lambda j: p2(j, False, core).wait_recv())

    by_core(p2_take)

    def code_of(r):
        return ((r >> 1) & 3) * 4096 + (r >> 4) * 4 + ((r >> 3) & 1) * 2 + (r & 1)

    keys = got[:, :, :, HD : 2 * HD].reshape(1024, HD)
    lane_zero = (iota((8, HD), 1) == 0).astype(F32).astype(BF)
    lead_key = dot(lane_zero, keys, NT)[0:1]
    key_code = jnp.where(lead_key < 0.75 * EMPTY, code_of(iota((8, 1024), 1))[0:1], 1 << 20)

    def cluster_rows(last, i):
        keys = got[: last // 128, :, :, HD : 2 * HD].reshape(last, HD)
        values = got[: last // 128, :, :, 2 * HD :].reshape(last, HD)
        query = got[pl.ds(2 * i, 2), :, :, 0:HD].reshape(256, HD)
        scores = dot(query, keys, NT) * SCALE
        ahead = code_of(iota((256, HD), 0) + i * 256)[:, 0:1] - key_code[:, :last]
        scores = jnp.where((ahead >= 0) & (ahead < 256), scores, NEVER)
        raised = jnp.exp(scores - jnp.max(scores, axis=1, keepdims=True))
        weights = (raised * (1.0 / jnp.sum(raised, axis=1, keepdims=True))).astype(BF)
        answer[pl.ds(2 * i, 2)] = dot(weights, values, NN).astype(BF).reshape(2, SIDE, 16, HD)

    each(0, 2, functools.partial(cluster_rows, 512))
    each(2, 4, functools.partial(cluster_rows, 1024))

    def q1(j, sending, core):
        there, here = rem(w + j, SIDE), rem(w + SIDE - j, SIDE)
        src = answer.at[there] if core == 0 else answer.at[:, there]
        dst = back.at[w] if sending else back.at[here]
        return to_seq(src, dst, q1_s.at[j], q1_r.at[j], seq_uw(u, there))

    def q1_start(core):
        each(1, SIDE, lambda j: q1(j, True, core).start())

        def keep(i):
            back[w, i] = answer[w, i] if core == 0 else answer[i, w]

        each(0, SIDE, keep)

    by_core(q1_start)


    each(1, SIDE, lambda j: q1(j, False, 0).wait_recv())

    def q2(j, sending):
        there, here = rem(u + j, SIDE), rem(u + SIDE - j, SIDE)
        dst = final.at[u] if sending else final.at[here]
        return to_seq(back.at[:, there], dst, q2_s.at[j], q2_r.at[j], seq_uw(there, w))

    each(1, SIDE, lambda j: q2(j, True).start())

    def keep_final(i):
        final[u, i] = back[i, u]

    each(0, SIDE, keep_final)

    ring_step(3)

    each(1, SIDE, lambda j: q2(j, False).wait_recv())
    tokens = dot(place[...], final[...].reshape(1024, HD), TN).astype(BF)
    picked[0] = tokens[:TOK]
    picked[1] = tokens[TOK:]
    ax_send = to_seq(picked.at[oc], routed_out.at[c], ax_s, ax_r, sibling)
    ax_send.start()
    routed_out[c] = picked[c]
    to_seq(picked.at[oc], routed_out.at[oc], ax_s, ax_r, sibling).wait_recv()
    acts[:, 0:HD] = routed_out[0]
    acts[:, HD : 2 * HD] = routed_out[1]

    def send_a(yy):
        head, e = div(yy, 2), rem(yy, 2)
        return to_head(
            stage_a.at[yy], arrived.at[h, e, :, e], xa_s.at[yy],
            xa_r.at[rem(head + GROUPS - h, GROUPS), e], head,
        )

    def send_b(pair, head):
        q, par = div(pair, 2), rem(pair, 2)
        return to_head(
            stage_b.at[pair, head], arrived.at[h, 1 - par, q, par], xb_s.at[pair, head],
            xb_r.at[rem(head + GROUPS - h, GROUPS), pair], jnp.int32(head),
        )

    def project_a(at):
        yy = rem(at + SIDE, SIDE)
        head, e = div(yy, 2), rem(yy, 2)
        rows = jnp.concatenate([wt[head, e, 0, e], wt[head, e, 1, e]], axis=0)
        share = dot(acts[...], rows, NT).astype(BF)
        stage_a[yy, 0] = share[:, :HD]
        stage_a[yy, 1] = share[:, HD:]

        @pl.when(head == h)
        def _():
            arrived[h, e, 0, e] = share[:, :HD]
            arrived[h, e, 1, e] = share[:, HD:]

        @pl.when(head != h)
        def _():
            send_a(yy).start()

    def project_b(at):
        pair = rem(at + 4, 4)
        q, par = div(pair, 2), rem(pair, 2)
        rows = jnp.concatenate([wt[i, 1 - par, q, par] for i in range(4)], axis=0)
        share = dot(acts[...], rows, NT).astype(BF)
        for head in range(GROUPS):
            tile = share[:, head * HD : (head + 1) * HD]
            stage_b[pair, head] = tile

            @pl.when(h == head)
            def _():
                arrived[h, 1 - par, q, par] = tile

            @pl.when(h != head)
            def _():
                send_b(pair, head).start()

    zb, zp = rem(z, 2), div(z, 2)
    turn = 1 - 2 * zb

    def swing(t):
        return div(t + 1, 2) * (1 - 2 * rem(t, 2))

    def share_out(k):
        for step in range(SIDE // 2 + 1):

            @pl.when(k == step)
            def _():
                if step >= 3:
                    ring_step(step + 1)
                sib_wait(step)

        @pl.when(k > 0)
        def _():
            project_b(zp + turn * swing(k - 1) + 4)

        each(jnp.maximum(2 * k - 1, 0), jnp.minimum(2 * k + 1, SIDE), lambda t: project_a(y + swing(t)))

    each(0, SIDE // 2 + 1, share_out)

    for j in range(1, GROUPS):
        src = rem(h + GROUPS - j, GROUPS)
        for e in range(2):
            to_head(
                stage_a.at[0], arrived.at[src, e, :, e], xa_s.at[0], xa_r.at[j, e], src
            ).wait_recv()
        for pair in range(4):
            q, par = pair // 2, pair % 2
            to_head(
                stage_b.at[0, 0], arrived.at[src, 1 - par, q, par], xb_s.at[0, 0], xb_r.at[j, pair], src
            ).wait_recv()

    def add_up(n):
        e, q, par = div(n, 4), rem(div(n, 2), 2), rem(n, 2)
        total = arrived[0, e, q, par].astype(F32)
        for g in range(1, GROUPS):
            total = total + arrived[g, e, q, par].astype(F32)
        out[:, pl.ds(pl.multiple_of(n * HD, HD), HD)] = total.astype(BF)

    each(0, 8, add_up)

    for copy in a0(c):
        copy.wait_send()

    @pl.when(s < 2 * SIDE * SIDE - 1)
    def _():
        halo_copy.wait_send()

    @pl.when(jnp.logical_not(holds))
    def _():
        for copy in w_send:
            copy.wait_send()

    def left(j):
        p1(j, True).wait_send()
        q2(j, True).wait_send()

    each(1, SIDE, left)

    def drain(core):
        def left(j):
            p2(j, True, core).wait_send()
            q1(j, True, core).wait_send()

        each(1, SIDE, left)

        @pl.when(holds)
        def _():
            each(1, SIDE, lambda j: w1(j, core, True).wait_send())

        for k in range(1, SIDE // 2 + 1):
            for way in range(2):
                ring(k, way, core, True).wait_send()
        for k in range(SIDE // 2 + 1):
            for way in ways(k):
                sib(k, way, core).wait_send()

    by_core(drain)
    ax_send.wait_send()
    def left_a(yy):
        @pl.when(h != div(yy, 2))
        def _():
            send_a(yy).wait_send()

    each(0, SIDE, left_a)

    for head in range(GROUPS):

        @pl.when(h != head)
        def _():
            each(0, 4, lambda pair: send_b(pair, head).wait_send())


def on_device(routed_qkv, local_qkv, cluster_ids, wo_routed, wo_local):
    sems = [
        (7,), (4,), (4,), (), (), (2,), (2,), (8,), (8,), (8,), (8,), (8,), (8,),
        (5, 2), (5, 2), (5, 2), (5, 2), (8,), (8,), (8,), (8,), (), (),
        (8,), (4, 2), (4, 4), (4, 4),
    ]
    scratch = [
        pltpu.VMEM((2, TOK, 4 * HD), BF),
        pltpu.VMEM((2, 1, TOK), I32),
        pltpu.VMEM((3, TOK, LOCAL * HD), BF),
        pltpu.VMEM((1024, 2 * TOK), BF),
        pltpu.VMEM((8, 8, 16, 3 * HD), BF),
        pltpu.VMEM((8, 8, 16, 3 * HD), BF),
        pltpu.VMEM((8, 8, 16, 3 * HD), BF),
        pltpu.VMEM((8, 8, 16, HD), BF),
        pltpu.VMEM((8, 8, 16, HD), BF),
        pltpu.VMEM((8, 8, 16, HD), BF),
        pltpu.VMEM((2, TOK, HD), BF),
        pltpu.VMEM((2, TOK, HD), BF),
        pltpu.VMEM((TOK, 8 * HD), BF),
        pltpu.VMEM((2, TOK, LOCAL * HD), BF),
        pltpu.VMEM((4, 2, 2, 2, 128, 8 * HD), BF),
        pltpu.VMEM((8, 2, TOK, HD), BF),
        pltpu.VMEM((4, 4, TOK, HD), BF),
        pltpu.VMEM((4, 2, 2, 2, TOK, HD), BF),
    ]
    scratch += [pltpu.SemaphoreType.DMA(shape) if shape else pltpu.SemaphoreType.DMA for shape in sems]
    return pl.pallas_call(
        kernel,
        out_shape=jax.ShapeDtypeStruct((TOK, 1024), BF),
        in_specs=[pl.BlockSpec(memory_space=pltpu.HBM)] * 5,
        out_specs=pl.BlockSpec(memory_space=pltpu.VMEM),
        scratch_shapes=scratch,
        compiler_params=pltpu.CompilerParams(
            collective_id=0, has_side_effects=True, vmem_limit_bytes=60 * 2**20
        ),
        cost_estimate=pl.CostEstimate(flops=4 * 10**9, bytes_accessed=3 * 2**20, transcendentals=2 * 10**6),
    )(routed_qkv, local_qkv, cluster_ids.transpose(0, 2, 1), wo_routed.T, wo_local.T)


def solution(mesh):
    placed = (
        P(None, "seq", "head"),
        P(None, "seq", "head"),
        P("head", "seq", None),
        P("head", "seq"),
        P("head", "seq"),
    )
    return jax.shard_map(
        on_device, mesh=mesh, in_specs=placed, out_specs=P("seq", "head"), check_vma=False
    )
```

time: 110 us -> 113 us (1.027)
  Pallas kernels: 103 us -> 110 us
  local copies, waits for them, and re-layouts: 5.54 us -> 1.87 us
    pallas_call x1, Pallas kernels: 103 us -> 110 us  [on_device(): pl.pallas_call(kernel, out_shape=jax.ShapeDtypeStruct((TOK, 1024), BF), i...]
    unnamed x8 -> x1, local copies, waits for them, and re-layouts: 5.54 us -> 1.87 us
where the time goes in v3:
time: 113 us; the launch traced here: 111 us
  Pallas kernels  110 us (97%)
  local copies, waits for them, and re-layouts  1.87 us (2%)
    pallas_call x1, Pallas kernels, on_device(): pl.pallas_call(kernel, out_shape=jax.ShapeDtypeStruct((TOK, 1024), BF), i...  110 us

profile of v3, /device:TPU:1, one launch (start us, length us, event | category | flops | bytes accessed | tf_op | source)
XLA Modules:
  0.0 111.4 jit_solution(11976760268993824100)
XLA Ops:
  0.0 109.6 %shard_map.55 = bf16[256,1024]{1,0:T(8,128)(2,1)} custom-call(bf16[3,256,256]{2,1,0:T(8,128)(2,1)} %routed.1, bf16[3,256,768]{2,1,0:T(8,128)(2,1)} %local_in.1, s32[2,1,256]{2,1,0:T(1,128)} %bitcast.5, bf16[32,256]{1,0:T(8,128)(2,1)} %bitcast.4, bf16[32,768]{1,0:T(8,128)(2,1)} %bitcast.3), custom_call_target="tpu_custom_call" | custom-call | flops 4000000000 | bytes 3145728 | tf_op jit(solution)/shard_map/pallas_call | solution.py:597
  109.6 1.9 %copy.7 = bf16[256,1024]{1,0:T(8,128)(2,1)} copy(bf16[256,1024]{1,0:T(8,128)(2,1)} %shard_map.55) | data formatting | bytes 1048576

commit v4 on v3

v4 whole, which is shorter than its diff:
```python
import functools
import math

import jax
import jax.numpy as jnp
from jax import lax
from jax.experimental import pallas as pl
from jax.experimental.pallas import tpu as pltpu
from jax.sharding import PartitionSpec as P

HD = 128
TOK = 256
LOCAL = 6
SIDE = 8
GROUPS = 4
EMPTY = 128.0
NEVER = -1e30
SCALE = 1.0 / math.sqrt(HD)
BF = jnp.bfloat16
F32 = jnp.float32
I32 = jnp.int32
NT = (((1,), (1,)), ((), ()))
NN = (((1,), (0,)), ((), ()))
TN = (((0,), (0,)), ((), ()))


def dot(a, b, dims):
    return lax.dot_general(a, b, dims, preferred_element_type=F32)


def iota(shape, axis):
    return lax.broadcasted_iota(I32, shape, axis)


def each(low, high, body):
    for j in range(low, high):
        body(j)


def div(a, b):
    if isinstance(a, int):
        return a // b
    return lax.div(a, jnp.int32(b))


def rem(a, b):
    if isinstance(a, int):
        return a % b
    return lax.rem(a, jnp.int32(b))


def kernel(
    routed, local_in, ids, wr, wl, out,
    own_x, own_ids, local, place, sent, via, got, answer, back, final, picked, acts, routed_acts, halo,
    wt, summed,
    in_s, a0_s, a0_r, halo_s, halo_r, wx_s, wx_r, p1_s, p1_r, p2_s, p2_r, w1_s, w1_r,
    ring_s, ring_r, sib_s, sib_r, q1_s, q1_r, q2_s, q2_r, xl_s, xl_r, xr_s, xr_r,
):
    h = lax.axis_index("head")
    s = lax.axis_index("seq")
    c = rem(s, 2)
    oc = 1 - c
    chip = div(s, 2)
    z = rem(chip, SIDE)
    y = div(chip, SIDE)
    u = z * oc + y * c
    w = y * oc + z * c
    sibling = s + 1 - 2 * c

    def seq_yz(yy, zz):
        return (yy * SIDE + zz) * 2 + c

    def seq_uw(uu, ww):
        return seq_yz(ww * oc + uu * c, uu * oc + ww * c)

    def to_seq(src, dst, ss, rs, seq):
        return pltpu.make_async_remote_copy(
            src_ref=src, dst_ref=dst, send_sem=ss, recv_sem=rs,
            device_id={"seq": seq}, device_id_type=pl.DeviceIdType.MESH,
        )

    def to_any(src, dst, ss, rs, seq, head):
        return pltpu.make_async_remote_copy(
            src_ref=src, dst_ref=dst, send_sem=ss, recv_sem=rs,
            device_id={"seq": seq, "head": head}, device_id_type=pl.DeviceIdType.MESH,
        )

    def hello(seq, head):
        pl.semaphore_signal(
            barrier, inc=1, device_id={"seq": seq, "head": head}, device_id_type=pl.DeviceIdType.MESH
        )

    def w_target(r):
        return div(y, 2), rem(y, 2) * 4 + c * 2 + r, div(h, 2)

    def w_source(i):
        return 2 * c + i, 2 * h + div(y, 4), div(rem(y, 4), 2)

    def target_is_me(r):
        head, row, core = w_target(r)
        return (head == h) & (row == y) & (core == c)

    def source_is_me(i):
        head, row, core = w_source(i)
        return (head == h) & (row == y) & (core == c)

    barrier = pltpu.get_barrier_semaphore()

    def greet(j):
        for target in (seq_uw(rem(u + j, SIDE), w), seq_uw(u, rem(w + j, SIDE))):
            pl.semaphore_signal(barrier, inc=1, device_id={"seq": target}, device_id_type=pl.DeviceIdType.MESH)

    each(1, SIDE, greet)
    pl.semaphore_signal(barrier, inc=1, device_id={"seq": sibling}, device_id_type=pl.DeviceIdType.MESH)
    for j in range(1, GROUPS):
        hello(s, rem(h + j, GROUPS))
        hello(sibling, rem(h + j, GROUPS))
    for i in range(2):
        head, row, core = w_source(i)

        @pl.when(jnp.logical_not(source_is_me(i)))
        def _():
            hello((row * SIDE + z) * 2 + core, head)

    @pl.when((c == 0) & (s > 0))
    def _():
        pl.semaphore_signal(barrier, inc=1, device_id={"seq": s - 1}, device_id_type=pl.DeviceIdType.MESH)

    selves = jnp.where(target_is_me(0) | target_is_me(1), 1, 0)
    expected = 2 * (SIDE - 1) + 1 + 2 * (GROUPS - 1) + 2
    pl.semaphore_wait(barrier, expected + c * (1 - div(s, 2 * SIDE * SIDE - 1)) - selves)

    def lanes(first, count):
        return pl.ds(pl.multiple_of(first, HD), count)

    pieces = ((wr, 0, 2 * HD), (wl, 4 * HD, LOCAL * HD))

    def w_landing(row, head, piece):
        _, first, count = pieces[piece]
        at = lanes(div(head, 2) * 16 * HD + first + rem(head, 2) * count, count)
        return wt.at[div(row, 4), z, rem(row, 4), :, at]

    def w_send(r, piece):
        head, row, core = w_target(r)
        src = pieces[piece][0].at[pl.ds(r * 16, 16)]
        return to_any(
            src, w_landing(row, h, piece), wx_s.at[r, piece], wx_r.at[rem(h, 2), piece],
            (row * SIDE + z) * 2 + core, head,
        )

    def w_keep(r, piece):
        src = pieces[piece][0].at[pl.ds(r * 16, 16)]
        return pltpu.make_async_copy(src, w_landing(w_target(r)[1], h, piece), in_s.at[piece])

    def w_take(i, piece):
        head, row, core = w_source(i)
        src = pieces[piece][0].at[pl.ds(0, 16)]
        return to_any(
            src, w_landing(y, head, piece), wx_s.at[0, piece], wx_r.at[i, piece],
            (row * SIDE + z) * 2 + core, head,
        )

    for r in range(2):
        me = target_is_me(r)

        @pl.when(me)
        def _():
            for piece in range(2):
                w_keep(r, piece).start()

        @pl.when(jnp.logical_not(me))
        def _():
            for piece in range(2):
                w_send(r, piece).start()

    def head_rows(j, core):
        return routed.at[j, :, pl.ds(pl.multiple_of(core * HD, HD), HD)]

    def a0(core):
        copies = [
            to_seq(head_rows(j, oc), own_x.at[core, :, pl.ds(j * HD, HD)], a0_s.at[j], a0_r.at[j], sibling)
            for j in range(3)
        ]
        return copies + [to_seq(ids.at[oc], own_ids.at[core], a0_s.at[3], a0_r.at[3], sibling)]

    for copy in a0(c):
        copy.start()
    own = [
        pltpu.make_async_copy(head_rows(j, c), own_x.at[c, :, pl.ds(j * HD, HD)], in_s.at[2 + j])
        for j in range(3)
    ]
    own.append(pltpu.make_async_copy(ids.at[c], own_ids.at[c], in_s.at[5]))
    own.append(pltpu.make_async_copy(local_in, local, in_s.at[6]))
    for copy in own:
        copy.start()
    halo_copy = to_seq(local_in.at[pl.ds(1, 2)], halo, halo_s, halo_r, s + 1)
    own_x[:, :, 3 * HD :] = jnp.ones((2, TOK, HD), BF)

    def block_of(core, yy, zz):
        return wt.at[div(yy, 4), zz, rem(yy, 4), :, pl.ds(core * 16 * HD, 16 * HD)]

    def w1(j, core, sending):
        if core == 0:
            target = seq_yz(y, rem(z + j, SIDE))
            here = rem(z + SIDE - j, SIDE)
            blk = block_of(core, y, z) if sending else block_of(core, y, here)
        else:
            target = seq_yz(rem(y + j, SIDE), z)
            here = rem(y + SIDE - j, SIDE)
            blk = block_of(core, y, z) if sending else block_of(core, here, z)
        return to_seq(blk, blk, w1_s.at[j], w1_r.at[j], target)

    def by_core(body):
        for core in range(2):
            pl.when(c == core)(functools.partial(body, core))

    for copy in own[:4]:
        copy.wait()
    for copy in a0(oc):
        copy.wait_recv()

    def rows_of(b):
        cluster = own_ids[b]
        name = cluster.astype(F32)
        first_row = jnp.where(iota((8, TOK), 0) == 0, jnp.broadcast_to(name, (8, TOK)), 0.0).astype(BF)
        down = dot(first_row, jnp.ones((8, TOK), BF), TN)
        earlier = (down == name) & (iota((TOK, TOK), 0) < iota((TOK, TOK), 1))
        rank = jnp.sum(jnp.where(earlier, 1.0, 0.0), axis=0, keepdims=True).astype(I32)
        owner = cluster >> 2
        turned = (owner & 7) * SIDE + (owner >> 3)
        goes = turned * oc + owner * c
        return goes * 16 + b * 8 + (cluster & 3) * 2 + rank

    slot = jnp.concatenate([rows_of(0), rows_of(1)], axis=1)
    both = own_x[...].reshape(2 * TOK, 4 * HD)

    def fill(i):
        hot = (iota((256, 2 * TOK), 0) + i * 256 == slot).astype(F32).astype(BF)
        place[pl.ds(i * 256, 256)] = hot
        rows = dot(hot, both, NN)
        lead = (1.0 - rows[:, 3 * HD :]) * EMPTY
        rows = jnp.concatenate([rows[:, :HD], rows[:, HD : 2 * HD] + lead, rows[:, 2 * HD : 3 * HD]], axis=1)
        sent[pl.ds(2 * i, 2)] = rows.astype(BF).reshape(2, SIDE, 16, 3 * HD)

    each(0, 4, fill)

    def p1(j, sending):
        there, here = rem(u + j, SIDE), rem(u + SIDE - j, SIDE)
        dst = via.at[u] if sending else via.at[here]
        return to_seq(sent.at[there], dst, p1_s.at[j], p1_r.at[j], seq_uw(there, w))

    each(1, SIDE, lambda j: p1(j, True).start())
    via[u] = sent[u]

    for i in range(2):
        me = source_is_me(i)
        for piece in range(2):

            @pl.when(me)
            def _():
                r = rem(y, 2)
                for value in range(2):

                    @pl.when(r == value)
                    def _():
                        w_keep(value, piece).wait()

            @pl.when(jnp.logical_not(me))
            def _():
                w_take(i, piece).wait_recv()

    def w1_start(core):
        each(1, SIDE, lambda j: w1(j, core, True).start())

    by_core(w1_start)

    @pl.when(s < 2 * SIDE * SIDE - 1)
    def _():
        halo_copy.start()

    def w1_take(core):
        each(1, SIDE, lambda j: w1(j, core, False).wait_recv())

    by_core(w1_take)

    def blocks(core, place_on, first=0, count=16 * HD):
        at = rem(place_on + SIDE, SIDE)
        part = pl.ds(core * 16 * HD + first, count)
        if core == 0:
            return wt.at[div(at, 4), :, rem(at, 4), :, part]
        return wt.at[:, at, :, :, part]

    def ring(k, way, core, sending):
        coord = y if core == 0 else z
        sign = 1 - 2 * way
        if sending:
            at = coord - sign * (k - 1)
        else:
            at = coord - sign * k
        blk = blocks(core, at, way * 8 * HD, 8 * HD) if k == SIDE // 2 else blocks(core, at)
        to = rem(coord + sign + SIDE, SIDE)
        target = seq_yz(to, z) if core == 0 else seq_yz(y, to)
        return to_seq(blk, blk, ring_s.at[k, way], ring_r.at[k, way], target)

    def sib(k, way, path):
        coord = y if path == 0 else z
        blk = blocks(path, coord - (1 - 2 * way) * k)
        return to_seq(blk, blk, sib_s.at[k, way], sib_r.at[k, way], sibling)

    def ways(k):
        return (0,) if k in (0, SIDE // 2) else (0, 1)

    def ring_step(k):
        def body(core):
            if k > 1:
                for way in range(2):
                    ring(k - 1, way, core, False).wait_recv()
            if k <= SIDE // 2:
                for way in range(2):
                    ring(k, way, core, True).start()
            for way in ways(k - 1):
                sib(k - 1, way, core).start()

        by_core(body)

    def sib_wait(k):
        def body(core):
            for way in ways(k):
                sib(k, way, 1 - core).wait_recv()

        by_core(body)

    ring_step(1)

    each(1, SIDE, lambda j: p1(j, False).wait_recv())

    def p2(j, sending, core):
        there, here = rem(w + j, SIDE), rem(w + SIDE - j, SIDE)
        at = w if sending else here
        dst = got.at[at] if core == 0 else got.at[:, at]
        return to_seq(via.at[:, there], dst, p2_s.at[j], p2_r.at[j], seq_uw(u, there))

    def p2_start(core):
        each(1, SIDE, lambda j: p2(j, True, core).start())

        def keep(i):
            if core == 0:
                got[w, i] = via[i, w]
            else:
                got[i, w] = via[i, w]

        each(0, SIDE, keep)

    by_core(p2_start)

    own[4].wait()

    @pl.when(s > 0)
    def _():
        halo_copy.wait_recv()

    @pl.when(s == 0)
    def _():
        halo[...] = jnp.zeros_like(halo)

    own_side = iota((TOK, TOK), 1) <= iota((TOK, TOK), 0)
    shift = jnp.where(s > 0, jnp.float32(0.0), jnp.float32(NEVER))

    def window(n):
        cols = pl.ds(n * HD, HD)
        query = local[0, :, cols]
        here = dot(query, local[1, :, cols], NT) * SCALE
        before = dot(query, halo[0, :, cols], NT) * SCALE + shift
        scores = jnp.where(own_side, here, before)
        raised = jnp.exp(scores - jnp.max(scores, axis=1, keepdims=True))
        weights = raised * (1.0 / jnp.sum(raised, axis=1, keepdims=True))
        near = jnp.where(own_side, weights, 0.0).astype(BF)
        far = jnp.where(own_side, 0.0, weights).astype(BF)
        result = dot(near, local[2, :, cols], NN) + dot(far, halo[1, :, cols], NN)
        acts[h, :, pl.ds(n * HD, HD)] = result.astype(BF)

    each(0, LOCAL, window)

    def xl(j, sending):
        there, here = rem(h + j, GROUPS), rem(h + GROUPS - j, GROUPS)
        dst = acts.at[h] if sending else acts.at[here]
        return to_any(acts.at[h], dst, xl_s.at[j], xl_r.at[j], s, there)

    each(1, GROUPS, lambda j: xl(j, True).start())

    ring_step(2)

    def p2_take(core):
        each(1, SIDE, lambda j: p2(j, False, core).wait_recv())

    by_core(p2_take)

    def code_of(r):
        return ((r >> 1) & 3) * 4096 + (r >> 4) * 4 + ((r >> 3) & 1) * 2 + (r & 1)

    keys = got[:, :, :, HD : 2 * HD].reshape(1024, HD)
    lane_zero = (iota((8, HD), 1) == 0).astype(F32).astype(BF)
    lead_key = dot(lane_zero, keys, NT)[0:1]
    key_code = jnp.where(lead_key < 0.75 * EMPTY, code_of(iota((8, 1024), 1))[0:1], 1 << 20)

    def cluster_rows(last, i):
        keys = got[: last // 128, :, :, HD : 2 * HD].reshape(last, HD)
        values = got[: last // 128, :, :, 2 * HD :].reshape(last, HD)
        query = got[pl.ds(2 * i, 2), :, :, 0:HD].reshape(256, HD)
        scores = dot(query, keys, NT) * SCALE
        ahead = code_of(iota((256, HD), 0) + i * 256)[:, 0:1] - key_code[:, :last]
        scores = jnp.where((ahead >= 0) & (ahead < 256), scores, NEVER)
        raised = jnp.exp(scores - jnp.max(scores, axis=1, keepdims=True))
        weights = (raised * (1.0 / jnp.sum(raised, axis=1, keepdims=True))).astype(BF)
        answer[pl.ds(2 * i, 2)] = dot(weights, values, NN).astype(BF).reshape(2, SIDE, 16, HD)

    for i in range(4):
        cluster_rows((i + 1) * 256, i)

    def q1(j, sending, core):
        there, here = rem(w + j, SIDE), rem(w + SIDE - j, SIDE)
        src = answer.at[there] if core == 0 else answer.at[:, there]
        dst = back.at[w] if sending else back.at[here]
        return to_seq(src, dst, q1_s.at[j], q1_r.at[j], seq_uw(u, there))

    def q1_start(core):
        each(1, SIDE, lambda j: q1(j, True, core).start())

        def keep(i):
            back[w, i] = answer[w, i] if core == 0 else answer[i, w]

        each(0, SIDE, keep)

    by_core(q1_start)


    ring_step(3)

    each(1, SIDE, lambda j: q1(j, False, 0).wait_recv())

    def q2(j, sending):
        there, here = rem(u + j, SIDE), rem(u + SIDE - j, SIDE)
        dst = final.at[u] if sending else final.at[here]
        return to_seq(back.at[:, there], dst, q2_s.at[j], q2_r.at[j], seq_uw(there, w))

    each(1, SIDE, lambda j: q2(j, True).start())

    def keep_final(i):
        final[u, i] = back[i, u]

    each(0, SIDE, keep_final)

    ring_step(4)

    each(1, SIDE, lambda j: q2(j, False).wait_recv())
    tokens = dot(place[...], final[...].reshape(1024, HD), TN).astype(BF)
    picked[0] = tokens[:TOK]
    picked[1] = tokens[TOK:]

    def xr(j, b, sending):
        there, here = rem(h + j, GROUPS), rem(h + GROUPS - j, GROUPS)
        own_side = c * (1 - b) + oc * b
        to = s * (1 - b) + sibling * b
        if sending:
            src, dst = picked.at[own_side], routed_acts.at[h, c]
        else:
            src, dst = picked.at[0], routed_acts.at[here, own_side]
        return to_any(src, dst, xr_s.at[j, b], xr_r.at[j, b], to, there if sending else here)

    for j in range(GROUPS):
        for b in range(2):
            if j or b:
                xr(j, b, True).start()
    routed_acts[h, c] = picked[c]

    ring_step(5)
    for k in range(SIDE // 2 + 1):
        sib_wait(k)
    each(1, GROUPS, lambda j: xl(j, False).wait_recv())

    def rows_at(first, count):
        return wt[:, :, :, :, first : first + count].reshape(1024, count)

    total = jnp.zeros((TOK, 1024), F32)
    for g in range(GROUPS):
        total = total + dot(acts[g], rows_at(g // 2 * 16 * HD + (4 + g % 2 * LOCAL) * HD, LOCAL * HD), NT)
    summed[...] = total
    for j in range(GROUPS):
        for b in range(2):
            if j or b:
                xr(j, b, False).wait_recv()
    total = summed[...]
    for half in range(2):
        wide = jnp.concatenate([routed_acts[2 * half + g, n] for g in range(2) for n in range(2)], axis=1)
        total = total + dot(wide, rows_at(half * 16 * HD, 4 * HD), NT)
    out[...] = total.astype(BF)

    for copy in a0(c):
        copy.wait_send()

    @pl.when(s < 2 * SIDE * SIDE - 1)
    def _():
        halo_copy.wait_send()

    for r in range(2):

        @pl.when(jnp.logical_not(target_is_me(r)))
        def _():
            for piece in range(2):
                w_send(r, piece).wait_send()

    def left(j):
        p1(j, True).wait_send()
        q2(j, True).wait_send()

    each(1, SIDE, left)

    def drain(core):
        def left(j):
            p2(j, True, core).wait_send()
            q1(j, True, core).wait_send()

        each(1, SIDE, left)

        each(1, SIDE, lambda j: w1(j, core, True).wait_send())

        for k in range(1, SIDE // 2 + 1):
            for way in range(2):
                ring(k, way, core, True).wait_send()
        for k in range(SIDE // 2 + 1):
            for way in ways(k):
                sib(k, way, core).wait_send()

    by_core(drain)
    each(1, GROUPS, lambda j: xl(j, True).wait_send())
    for j in range(GROUPS):
        for b in range(2):
            if j or b:
                xr(j, b, True).wait_send()


def on_device(routed_qkv, local_qkv, cluster_ids, wo_routed, wo_local):
    sems = [
        (7,), (4,), (4,), (), (), (2, 2), (2, 2), (8,), (8,), (8,), (8,), (8,), (8,),
        (5, 2), (5, 2), (5, 2), (5, 2), (8,), (8,), (8,), (8,),
        (4,), (4,), (4, 2), (4, 2),
    ]
    scratch = [
        pltpu.VMEM((2, TOK, 4 * HD), BF),
        pltpu.VMEM((2, 1, TOK), I32),
        pltpu.VMEM((3, TOK, LOCAL * HD), BF),
        pltpu.VMEM((1024, 2 * TOK), BF),
        pltpu.VMEM((8, 8, 16, 3 * HD), BF),
        pltpu.VMEM((8, 8, 16, 3 * HD), BF),
        pltpu.VMEM((8, 8, 16, 3 * HD), BF),
        pltpu.VMEM((8, 8, 16, HD), BF),
        pltpu.VMEM((8, 8, 16, HD), BF),
        pltpu.VMEM((8, 8, 16, HD), BF),
        pltpu.VMEM((2, TOK, HD), BF),
        pltpu.VMEM((GROUPS, TOK, LOCAL * HD), BF),
        pltpu.VMEM((GROUPS, 2, TOK, HD), BF),
        pltpu.VMEM((2, TOK, LOCAL * HD), BF),
        pltpu.VMEM((2, 8, 4, 16, 32 * HD), BF),
        pltpu.VMEM((TOK, 1024), F32),
    ]
    scratch += [pltpu.SemaphoreType.DMA(shape) if shape else pltpu.SemaphoreType.DMA for shape in sems]
    return pl.pallas_call(
        kernel,
        out_shape=jax.ShapeDtypeStruct((TOK, 1024), BF),
        in_specs=[pl.BlockSpec(memory_space=pltpu.HBM)] * 5,
        out_specs=pl.BlockSpec(memory_space=pltpu.VMEM),
        scratch_shapes=scratch,
        compiler_params=pltpu.CompilerParams(
            collective_id=0, has_side_effects=True, vmem_limit_bytes=60 * 2**20
        ),
        cost_estimate=pl.CostEstimate(flops=4 * 10**9, bytes_accessed=3 * 2**20, transcendentals=2 * 10**6),
    )(routed_qkv, local_qkv, cluster_ids.transpose(0, 2, 1), wo_routed.T, wo_local.T)


def solution(mesh):
    placed = (
        P(None, "seq", "head"),
        P(None, "seq", "head"),
        P("head", "seq", None),
        P("head", "seq"),
        P("head", "seq"),
    )
    return jax.shard_map(
        on_device, mesh=mesh, in_specs=placed, out_specs=P("seq", "head"), check_vma=False
    )
```

time: 113 us -> 92.6 us (0.82); the launches traced: 111 us -> 92.4 us
  Pallas kernels: 110 us -> 90.5 us
    pallas_call x1, Pallas kernels: 110 us -> 90.5 us  [on_device(): pl.pallas_call(kernel, out_shape=jax.ShapeDtypeStruct((TOK, 1024), BF), i...]
where the time goes in v4:
time: 92.6 us; the launch traced here: 92.4 us
  Pallas kernels  90.5 us (98%)
  local copies, waits for them, and re-layouts  1.87 us (2%)
    pallas_call x1, Pallas kernels, on_device(): pl.pallas_call(kernel, out_shape=jax.ShapeDtypeStruct((TOK, 1024), BF), i...  90.5 us
    unnamed x1, local copies, waits for them, and re-layouts  1.87 us

profile of v4, /device:TPU:1, one launch (start us, length us, event | category | flops | bytes accessed | tf_op | source)
XLA Modules:
  0.0 92.4 jit_solution(14849232940350918698)
XLA Ops:
  0.0 90.5 %shard_map.55 = bf16[256,1024]{1,0:T(8,128)(2,1)} custom-call(bf16[3,256,256]{2,1,0:T(8,128)(2,1)} %routed.1, bf16[3,256,768]{2,1,0:T(8,128)(2,1)} %local_in.1, s32[2,1,256]{2,1,0:T(1,128)} %bitcast.5, bf16[32,256]{1,0:T(8,128)(2,1)} %bitcast.4, bf16[32,768]{1,0:T(8,128)(2,1)} %bitcast.3), custom_call_target="tpu_custom_call" | custom-call | flops 4000000000 | bytes 3145728 | tf_op jit(solution)/shard_map/pallas_call | solution.py:567
  90.5 1.9 %copy.7 = bf16[256,1024]{1,0:T(8,128)(2,1)} copy(bf16[256,1024]{1,0:T(8,128)(2,1)} %shard_map.55) | data formatting | bytes 1048576

commit v5 on v4

--- a/solution.py
+++ b/solution.py
@@ -133,6 +133,8 @@
     def lanes(first, count):
         return pl.ds(pl.multiple_of(first, HD), count)
 
+    halo_copy = to_seq(local_in.at[pl.ds(1, 2)], halo, halo_s, halo_r, s + 1)
+
     pieces = ((wr, 0, 2 * HD), (wl, 4 * HD, LOCAL * HD))
 
     def w_landing(row, head, piece):
@@ -193,7 +195,6 @@
     own.append(pltpu.make_async_copy(local_in, local, in_s.at[6]))
     for copy in own:
         copy.start()
-    halo_copy = to_seq(local_in.at[pl.ds(1, 2)], halo, halo_s, halo_r, s + 1)
     own_x[:, :, 3 * HD :] = jnp.ones((2, TOK, HD), BF)
 
     def block_of(core, yy, zz):
@@ -278,6 +279,7 @@
     def _():
         halo_copy.start()
 
+
     def w1_take(core):
         each(1, SIDE, lambda j: w1(j, core, False).wait_recv())
 
@@ -290,17 +292,19 @@
             return wt.at[div(at, 4), :, rem(at, 4), :, part]
         return wt.at[:, at, :, :, part]
 
-    def ring(k, way, core, sending):
+    def ring(k, way, part, core, sending):
         coord = y if core == 0 else z
         sign = 1 - 2 * way
-        if sending:
-            at = coord - sign * (k - 1)
-        else:
-            at = coord - sign * k
-        blk = blocks(core, at, way * 8 * HD, 8 * HD) if k == SIDE // 2 else blocks(core, at)
+        at = coord - sign * (k - 1) if sending else coord - sign * k
+        blk = blocks(core, at, part * 8 * HD, 8 * HD)
         to = rem(coord + sign + SIDE, SIDE)
         target = seq_yz(to, z) if core == 0 else seq_yz(y, to)
-        return to_seq(blk, blk, ring_s.at[k, way], ring_r.at[k, way], target)
+        return to_seq(blk, blk, ring_s.at[k, way, part], ring_r.at[k, way, part], target)
+
+    def goes(k, part, core):
+        if k < SIDE // 2:
+            return (0, 1)
+        return (part,) if core == 0 else (1,)
 
     def sib(k, way, path):
         coord = y if path == 0 else z
@@ -310,16 +314,17 @@
     def ways(k):
         return (0,) if k in (0, SIDE // 2) else (0, 1)
 
-    def ring_step(k):
+    def ring_step(k, part):
         def body(core):
             if k > 1:
-                for way in range(2):
-                    ring(k - 1, way, core, False).wait_recv()
+                for way in goes(k - 1, part, core):
+                    ring(k - 1, way, part, core, False).wait_recv()
             if k <= SIDE // 2:
-                for way in range(2):
-                    ring(k, way, core, True).start()
-            for way in ways(k - 1):
-                sib(k - 1, way, core).start()
+                for way in goes(k, part, core):
+                    ring(k, way, part, core, True).start()
+            if part == 1:
+                for way in ways(k - 1):
+                    sib(k - 1, way, core).start()
 
         by_core(body)
 
@@ -330,7 +335,8 @@
 
         by_core(body)
 
-    ring_step(1)
+    ring_step(1, 0)
+    ring_step(1, 1)
 
     each(1, SIDE, lambda j: p1(j, False).wait_recv())
 
@@ -352,6 +358,8 @@
         each(0, SIDE, keep)
 
     by_core(p2_start)
+    ring_step(2, 0)
+    ring_step(2, 1)
 
     own[4].wait()
 
@@ -388,7 +396,6 @@
 
     each(1, GROUPS, lambda j: xl(j, True).start())
 
-    ring_step(2)
 
     def p2_take(core):
         each(1, SIDE, lambda j: p2(j, False, core).wait_recv())
@@ -434,7 +441,8 @@
     by_core(q1_start)
 
 
-    ring_step(3)
+    ring_step(3, 0)
+    ring_step(3, 1)
 
     each(1, SIDE, lambda j: q1(j, False, 0).wait_recv())
 
@@ -450,7 +458,25 @@
 
     each(0, SIDE, keep_final)
 
-    ring_step(4)
+    ring_step(4, 0)
+    ring_step(4, 1)
+
+    def project(e, zh):
+        for part in range(2):
+            first = (part * 16 + 4) * HD
+            wide = jnp.concatenate([acts[2 * part], acts[2 * part + 1]], axis=1)
+            at = pl.ds(first, 2 * LOCAL * HD)
+            if part == 0:
+                rows = wt[e, :, :, :, at]
+            else:
+                rows = wt[:, pl.ds(zh * 4, 4), :, :, at]
+            share = dot(wide, rows.reshape(512, 2 * LOCAL * HD), NT)
+            for n in range(2):
+                piece = share[:, n * 256 : (n + 1) * 256]
+                if part == 0:
+                    summed[0, e, n] = piece
+                else:
+                    summed[1, n, zh] = piece
 
     each(1, SIDE, lambda j: q2(j, False).wait_recv())
     tokens = dot(place[...], final[...].reshape(1024, HD), TN).astype(BF)
@@ -473,27 +499,32 @@
                 xr(j, b, True).start()
     routed_acts[h, c] = picked[c]
 
-    ring_step(5)
-    for k in range(SIDE // 2 + 1):
+    for k in range(SIDE // 2):
         sib_wait(k)
     each(1, GROUPS, lambda j: xl(j, False).wait_recv())
-
-    def rows_at(first, count):
-        return wt[:, :, :, :, first : first + count].reshape(1024, count)
-
-    total = jnp.zeros((TOK, 1024), F32)
-    for g in range(GROUPS):
-        total = total + dot(acts[g], rows_at(g // 2 * 16 * HD + (4 + g % 2 * LOCAL) * HD, LOCAL * HD), NT)
-    summed[...] = total
+    project(div(y, 4), div(z, 4))
+
+    ring_step(5, 0)
+    ring_step(5, 1)
+    sib_wait(4)
+    project(1 - div(y, 4), 1 - div(z, 4))
     for j in range(GROUPS):
         for b in range(2):
             if j or b:
                 xr(j, b, False).wait_recv()
-    total = summed[...]
-    for half in range(2):
-        wide = jnp.concatenate([routed_acts[2 * half + g, n] for g in range(2) for n in range(2)], axis=1)
-        total = total + dot(wide, rows_at(half * 16 * HD, 4 * HD), NT)
-    out[...] = total.astype(BF)
+    wide = [
+        jnp.concatenate([routed_acts[2 * part + g, n] for g in range(2) for n in range(2)], axis=1)
+        for part in range(2)
+    ]
+    for e in range(2):
+        for zh in range(2):
+            total = summed[0, e, zh] + summed[1, e, zh]
+            for part in range(2):
+                first = part * 16 * HD
+                rows = wt[e, 4 * zh : 4 * zh + 4, :, :, first : first + 4 * HD].reshape(256, 4 * HD)
+                total = total + dot(wide[part], rows, NT)
+            first = e * 512 + zh * 256
+            out[:, first : first + 256] = total.astype(BF)
 
     for copy in a0(c):
         copy.wait_send()
@@ -525,8 +556,9 @@
         each(1, SIDE, lambda j: w1(j, core, True).wait_send())
 
         for k in range(1, SIDE // 2 + 1):
-            for way in range(2):
-                ring(k, way, core, True).wait_send()
+            for part in range(2):
+                for way in goes(k, part, core):
+                    ring(k, way, part, core, True).wait_send()
         for k in range(SIDE // 2 + 1):
             for way in ways(k):
                 sib(k, way, core).wait_send()
@@ -542,7 +574,7 @@
 def on_device(routed_qkv, local_qkv, cluster_ids, wo_routed, wo_local):
     sems = [
         (7,), (4,), (4,), (), (), (2, 2), (2, 2), (8,), (8,), (8,), (8,), (8,), (8,),
-        (5, 2), (5, 2), (5, 2), (5, 2), (8,), (8,), (8,), (8,),
+        (5, 2, 2), (5, 2, 2), (5, 2), (5, 2), (8,), (8,), (8,), (8,),
         (4,), (4,), (4, 2), (4, 2),
     ]
     scratch = [
@@ -561,7 +593,7 @@
         pltpu.VMEM((GROUPS, 2, TOK, HD), BF),
         pltpu.VMEM((2, TOK, LOCAL * HD), BF),
         pltpu.VMEM((2, 8, 4, 16, 32 * HD), BF),
-        pltpu.VMEM((TOK, 1024), F32),
+        pltpu.VMEM((2, 2, 2, TOK, 256), F32),
     ]
     scratch += [pltpu.SemaphoreType.DMA(shape) if shape else pltpu.SemaphoreType.DMA for shape in sems]
     return pl.pallas_call(

time: 92.6 us -> 89.4 us (0.965)
  Pallas kernels: 90.5 us -> 86.6 us
    pallas_call x1, Pallas kernels: 90.5 us -> 86.6 us  [on_device(): pl.pallas_call(kernel, out_shape=jax.ShapeDtypeStruct((TOK, 1024), BF), i...]
where the time goes in v5:
time: 89.4 us; the launch traced here: 88.5 us
  Pallas kernels  86.6 us (97%)
  local copies, waits for them, and re-layouts  1.87 us (2%)
    pallas_call x1, Pallas kernels, on_device(): pl.pallas_call(kernel, out_shape=jax.ShapeDtypeStruct((TOK, 1024), BF), i...  86.6 us
    unnamed x1, local copies, waits for them, and re-layouts  1.87 us

profile of v5, /device:TPU:1, one launch (start us, length us, event | category | flops | bytes accessed | tf_op | source)
XLA Modules:
  0.0 88.5 jit_solution(4323352099158546615)
XLA Ops:
  0.0 86.6 %shard_map.55 = bf16[256,1024]{1,0:T(8,128)(2,1)} custom-call(bf16[3,256,256]{2,1,0:T(8,128)(2,1)} %routed.1, bf16[3,256,768]{2,1,0:T(8,128)(2,1)} %local_in.1, s32[2,1,256]{2,1,0:T(1,128)} %bitcast.5, bf16[32,256]{1,0:T(8,128)(2,1)} %bitcast.4, bf16[32,768]{1,0:T(8,128)(2,1)} %bitcast.3), custom_call_target="tpu_custom_call" | custom-call | flops 4000000000 | bytes 3145728 | tf_op jit(solution)/shard_map/pallas_call | solution.py:599
  86.6 1.9 %copy.7 = bf16[256,1024]{1,0:T(8,128)(2,1)} copy(bf16[256,1024]{1,0:T(8,128)(2,1)} %shard_map.55) | data formatting | bytes 1048576

commit v6 on v5

--- a/solution.py
+++ b/solution.py
@@ -13,6 +13,7 @@
 LOCAL = 6
 SIDE = 8
 GROUPS = 4
+BOTH_WAYS = (4, 3, 5, 2, 6, 1, 7)
 EMPTY = 128.0
 NEVER = -1e30
 SCALE = 1.0 / math.sqrt(HD)
@@ -33,7 +34,7 @@
 
 
 def each(low, high, body):
-    for j in range(low, high):
+    for j in BOTH_WAYS if (low, high) == (1, SIDE) else range(low, high):
         body(j)
 
 

time: 89.4 us -> 88.9 us (level)
  no operation moved by 1% of the time
where the time goes in v6:
time: 88.9 us; the launch traced here: 88.8 us
  Pallas kernels  86.9 us (98%)
  local copies, waits for them, and re-layouts  1.87 us (2%)
    pallas_call x1, Pallas kernels, on_device(): pl.pallas_call(kernel, out_shape=jax.ShapeDtypeStruct((TOK, 1024), BF), i...  86.9 us
    unnamed x1, local copies, waits for them, and re-layouts  1.87 us

profile of v6, /device:TPU:1, one launch (start us, length us, event | category | flops | bytes accessed | tf_op | source)
XLA Modules:
  0.0 88.8 jit_solution(13027929086396042894)
XLA Ops:
  0.0 86.9 %shard_map.55 = bf16[256,1024]{1,0:T(8,128)(2,1)} custom-call(bf16[3,256,256]{2,1,0:T(8,128)(2,1)} %routed.1, bf16[3,256,768]{2,1,0:T(8,128)(2,1)} %local_in.1, s32[2,1,256]{2,1,0:T(1,128)} %bitcast.5, bf16[32,256]{1,0:T(8,128)(2,1)} %bitcast.4, bf16[32,768]{1,0:T(8,128)(2,1)} %bitcast.3), custom_call_target="tpu_custom_call" | custom-call | flops 4000000000 | bytes 3145728 | tf_op jit(solution)/shard_map/pallas_call | solution.py:600
  86.9 1.9 %copy.7 = bf16[256,1024]{1,0:T(8,128)(2,1)} copy(bf16[256,1024]{1,0:T(8,128)(2,1)} %shard_map.55) | data formatting | bytes 1048576

commit v7 on v6

--- a/solution.py
+++ b/solution.py
@@ -419,8 +419,8 @@
         ahead = code_of(iota((256, HD), 0) + i * 256)[:, 0:1] - key_code[:, :last]
         scores = jnp.where((ahead >= 0) & (ahead < 256), scores, NEVER)
         raised = jnp.exp(scores - jnp.max(scores, axis=1, keepdims=True))
-        weights = (raised * (1.0 / jnp.sum(raised, axis=1, keepdims=True))).astype(BF)
-        answer[pl.ds(2 * i, 2)] = dot(weights, values, NN).astype(BF).reshape(2, SIDE, 16, HD)
+        result = dot(raised.astype(BF), values, NN) * (1.0 / jnp.sum(raised, axis=1, keepdims=True))
+        answer[pl.ds(2 * i, 2)] = result.astype(BF).reshape(2, SIDE, 16, HD)
 
     for i in range(4):
         cluster_rows((i + 1) * 256, i)

time: 88.9 us -> 89.2 us (level)
  no operation moved by 1% of the time
where the time goes in v7:
time: 89.2 us; the launch traced here: 89 us
  Pallas kernels  87.1 us (98%)
  local copies, waits for them, and re-layouts  1.87 us (2%)
    pallas_call x1, Pallas kernels, on_device(): pl.pallas_call(kernel, out_shape=jax.ShapeDtypeStruct((TOK, 1024), BF), i...  87.1 us
    unnamed x1, local copies, waits for them, and re-layouts  1.87 us

profile of v7, /device:TPU:1, one launch (start us, length us, event | category | flops | bytes accessed | tf_op | source)
XLA Modules:
  0.0 89.0 jit_solution(17132249965468377768)
XLA Ops:
  0.0 87.1 %shard_map.55 = bf16[256,1024]{1,0:T(8,128)(2,1)} custom-call(bf16[3,256,256]{2,1,0:T(8,128)(2,1)} %routed.1, bf16[3,256,768]{2,1,0:T(8,128)(2,1)} %local_in.1, s32[2,1,256]{2,1,0:T(1,128)} %bitcast.5, bf16[32,256]{1,0:T(8,128)(2,1)} %bitcast.4, bf16[32,768]{1,0:T(8,128)(2,1)} %bitcast.3), custom_call_target="tpu_custom_call" | custom-call | flops 4000000000 | bytes 3145728 | tf_op jit(solution)/shard_map/pallas_call | solution.py:600
  87.1 1.9 %copy.7 = bf16[256,1024]{1,0:T(8,128)(2,1)} copy(bf16[256,1024]{1,0:T(8,128)(2,1)} %shard_map.55) | data formatting | bytes 1048576
